TPU v7x, 32 devices: a whole 2x2x4 slice. The times are simulated.
32 devices in a mesh: seq: 4 (over z), exp: 8 (over y, x, core).
Axes of the slice: x: 2, y: 2, z: 4, core: 2. Of those that a mesh axis runs over, the one named last changes fastest.
Arguments:
- tokens: bfloat16 [16, 512, 2048], P('exp', 'seq'), may hold values from -6 to 6
- cotangent: bfloat16 [16, 512, 2048], P('exp', 'seq'), may hold values from -6 to 6
- lengths: int32 [16], P('exp'), may hold values from 128 to 512, as said below
- adapter_choice: int32 [16, 8], P('exp'), may hold values from 0 to 1, as said below
- expert_ids: int32 [8, 4, 2, 128, 8], P('exp', 'seq'), may hold values from 0 to 31, all different within a row; in each aligned block of 256 rows (0 to 255, 256 to 511, ..., all dimensions but the last counted through in order) at most 96 rows name the same one
- gate_weights: float32 [8, 4, 2, 128, 8], P('exp', 'seq'), may hold values from 0.0625 to 0.1875
- attn_gain: float32 [2048], replicated, may hold values from 0.5 to 1.5
- moe_gain: float32 [2048], replicated, may hold values from 0.5 to 1.5
- query_gain: float32 [128], replicated, may hold values from 1 to 2
- key_gain: float32 [128], replicated, may hold values from 1 to 2
- w_qkv: bfloat16 [3, 2048, 2048], replicated, may hold values from -0.125 to 0.125
- w_out: bfloat16 [2048, 2048], replicated, may hold values from -0.5 to 0.5
- expert_gate: bfloat16 [32, 2048, 1024], P('exp'), may hold values from -0.125 to 0.125
- expert_up: bfloat16 [32, 2048, 1024], P('exp'), may hold values from -0.125 to 0.125
- expert_down: bfloat16 [32, 1024, 2048], P('exp'), may hold values from -1 to 1
- adapt_down: float32 [8, 4, 2048, 16], P(None, None, 'exp'), may hold values from -0.125 to 0.125
- first_down: float32 [8, 4, 2048, 16], P(None, None, 'exp'), may hold values from -1024 to 1024
- second_down: float32 [8, 4, 2048, 16], P(None, None, 'exp'), may hold values from 36864 to 147456
- adapt_up: float32 [8, 4, 16, 2048], P(None, None, None, 'exp'), may hold values from -1.5 to 1.5
- first_up: float32 [8, 4, 16, 2048], P(None, None, None, 'exp'), may hold values from -192 to 192
- second_up: float32 [8, 4, 16, 2048], P(None, None, None, 'exp'), may hold values from 1024 to 4096
Outputs:
- output: bfloat16 [16, 512, 2048], P('exp', 'seq')
- grad_input: float32 [16, 512, 2048], P('exp', 'seq')
- new_first_down: float32 [8, 4, 2048, 16], P(None, None, 'exp')
- new_second_down: float32 [8, 4, 2048, 16], P(None, None, 'exp')
- new_down: float32 [8, 4, 2048, 16], P(None, None, 'exp')
- new_first_up: float32 [8, 4, 16, 2048], P(None, None, None, 'exp')
- new_second_up: float32 [8, 4, 16, 2048], P(None, None, None, 'exp')
- new_up: float32 [8, 4, 16, 2048], P(None, None, None, 'exp')
Inputs may be any that keep to these rules, and one draw needn't show every extreme that they name: `lengths`: in each group of 2 sequences that share an index of exp, one, drawn from the seed, has length 512; the others are at least 128. `adapter_choice`: each row holds a single 1. `expert_ids`: each token names 8 different experts. Among the 256 tokens of one device (one index of exp and of seq) no expert is named more than 96 times, a bound that some block reaches.
All inputs are finite; a program needn't handle non-finite values.
Results may differ from a plain program's by a relative error of at most 0.025.
Values may be sent and summed in bfloat16 or wider, within the bound.
No kernel may reach another device: no remote copies, remote signals or barrier semaphores. Data moves between devices by JAX's collectives and lax.ppermute only.
A program may use at most 384 MiB of HBM per device.

v0:
```python
import jax
import jax.numpy as jnp
from jax import lax
from jax.sharding import PartitionSpec as P

HEAD = 128
STEP = 5


NORM_EPS = 1e-05
ROPE_BASE = 50000.0
ADAPTER_SCALE = 0.5
BETA_FIRST = 0.5
BETA_SECOND = 0.5
RATE_DOWN = 0.02
RATE_UP = 0.2
WEIGHT_DECAY = 0.01
ADAM_EPS = 1e-08
MASKED = -1e30


def rms_norm(values, gain):
    return values * lax.rsqrt(jnp.mean(values * values, axis=-1, keepdims=True) + NORM_EPS) * gain


def norm_back(values, gain, upstream):
    inverse = lax.rsqrt(jnp.mean(values * values, axis=-1, keepdims=True) + NORM_EPS)
    scaled = upstream * gain
    return inverse * scaled - values * (inverse * inverse * inverse) * jnp.mean(
        values * scaled, axis=-1, keepdims=True
    )


def rope_tables(positions):
    half_size = HEAD // 2
    frequency = ROPE_BASE ** (-(2.0 / HEAD) * jnp.arange(half_size, dtype=jnp.float32))
    angles = positions.astype(jnp.float32)[:, None] * frequency[None, :]
    return (jnp.cos(angles), jnp.sin(angles))


def rotate(values, cosine_table, sine_table):
    half_size = HEAD // 2
    front_half = values[..., :half_size]
    back_half = values[..., half_size:]
    cosine_wide = cosine_table[:, None, :]
    sine_wide = sine_table[:, None, :]
    return jnp.concatenate(
        [
            front_half * cosine_wide - back_half * sine_wide,
            back_half * cosine_wide + front_half * sine_wide,
        ],
        axis=-1,
    )


def rotate_back(grads, cosine_table, sine_table):
    half_size = HEAD // 2
    front_half = grads[..., :half_size]
    back_half = grads[..., half_size:]
    cosine_wide = cosine_table[:, None, :]
    sine_wide = sine_table[:, None, :]
    return jnp.concatenate(
        [
            front_half * cosine_wide + back_half * sine_wide,
            back_half * cosine_wide - front_half * sine_wide,
        ],
        axis=-1,
    )


def silu_value(values):
    return values * jax.nn.sigmoid(values)


def silu_slope(values):
    sigma = jax.nn.sigmoid(values)
    return sigma * (1.0 + values * (1.0 - sigma))


def adam_update(weight, gradient, first, second, step_rate):
    new_first = BETA_FIRST * first + (1.0 - BETA_FIRST) * gradient
    new_second = BETA_SECOND * second + (1.0 - BETA_SECOND) * gradient * gradient
    first_hat = new_first / (1.0 - BETA_FIRST**STEP)
    second_hat = new_second / (1.0 - BETA_SECOND**STEP)
    new_weight = weight - step_rate * (
        first_hat / (jnp.sqrt(second_hat) + ADAM_EPS) + WEIGHT_DECAY * weight
    )
    return (new_first, new_second, new_weight)


def local(
    tokens,
    cotangent,
    lengths,
    adapter_choice,
    expert_ids,
    gate_weights,
    attn_gain,
    moe_gain,
    query_gain,
    key_gain,
    w_qkv,
    w_out,
    expert_gate,
    expert_up,
    expert_down,
    adapt_down,
    first_down,
    second_down,
    adapt_up,
    first_up,
    second_up,
):
    group_count, shard_len, model_width = tokens.shape
    head_count = model_width // HEAD
    seq_devices = lax.axis_size("seq")
    total_len = shard_len * seq_devices
    positions = lax.axis_index("seq") * shard_len + jnp.arange(shard_len, dtype=jnp.int32)
    cosine_table, sine_table = rope_tables(positions)
    live_keys = jnp.arange(total_len, dtype=jnp.int32)[None, :] < lengths[:, None]
    own_live = positions[None, :] < lengths[:, None]
    live_rows = own_live.astype(jnp.float32)
    downs_full, ups_full = (
        lax.all_gather(adapt_down.astype(jnp.bfloat16), "exp", axis=2, tiled=True),
        lax.all_gather(adapt_up.astype(jnp.bfloat16), "exp", axis=3, tiled=True),
    )
    selector = adapter_choice.astype(jnp.bfloat16)
    down_pick = jnp.einsum(
        "gk,kpdr->gpdr", selector, downs_full, preferred_element_type=jnp.float32
    ).astype(jnp.bfloat16)
    up_pick = jnp.einsum(
        "gk,kprd->gprd", selector, ups_full, preferred_element_type=jnp.float32
    ).astype(jnp.bfloat16)
    inputs = tokens.astype(jnp.float32)
    normed = rms_norm(inputs, attn_gain).astype(jnp.bfloat16)

    def project(source, which_proj, weight):
        base_term = jnp.einsum("gsd,de->gse", source, weight, preferred_element_type=jnp.float32)
        middle = jnp.einsum(
            "gsd,gdr->gsr", source, down_pick[:, which_proj], preferred_element_type=jnp.float32
        ).astype(jnp.bfloat16)
        adapter_term = jnp.einsum(
            "gsr,gre->gse", middle, up_pick[:, which_proj], preferred_element_type=jnp.float32
        )
        return (base_term + ADAPTER_SCALE * adapter_term, middle)

    def project_back(upstream_low, source, middle, which_proj, weight):
        grad_middle = (
            ADAPTER_SCALE
            * jnp.einsum(
                "gse,gre->gsr",
                upstream_low,
                up_pick[:, which_proj],
                preferred_element_type=jnp.float32,
            )
        ).astype(jnp.bfloat16)
        grad_source = jnp.einsum(
            "gse,de->gsd", upstream_low, weight, preferred_element_type=jnp.float32
        )
        grad_source = grad_source + jnp.einsum(
            "gsr,gdr->gsd",
            grad_middle,
            down_pick[:, which_proj],
            preferred_element_type=jnp.float32,
        )
        grad_down_one = jnp.einsum(
            "gsd,gsr->gdr", source, grad_middle, preferred_element_type=jnp.float32
        )
        grad_up_one = ADAPTER_SCALE * jnp.einsum(
            "gsr,gse->gre", middle, upstream_low, preferred_element_type=jnp.float32
        )
        return (grad_source, grad_down_one, grad_up_one)

    def split_heads(values):
        return values.reshape(group_count, shard_len, head_count, HEAD)

    query_raw, query_mid = project(normed, 0, w_qkv[0])
    key_raw, key_mid = project(normed, 1, w_qkv[1])
    value_raw, value_mid = project(normed, 2, w_qkv[2])
    query_heads = split_heads(query_raw)
    key_heads = split_heads(key_raw)
    queries = rotate(rms_norm(query_heads, query_gain), cosine_table, sine_table).astype(
        jnp.bfloat16
    )
    key_rows = rotate(rms_norm(key_heads, key_gain), cosine_table, sine_table).astype(jnp.bfloat16)
    value_rows = split_heads(value_raw).astype(jnp.bfloat16)
    all_keys, all_values = (
        lax.all_gather(key_rows, "seq", axis=1, tiled=True),
        lax.all_gather(value_rows, "seq", axis=1, tiled=True),
    )
    score_scale = HEAD ** (-0.5)

    def scores_of(key_source):
        raw_scores = (
            jnp.einsum("gqhe,gkhe->ghqk", queries, key_source, preferred_element_type=jnp.float32)
            * score_scale
        )
        return jnp.where(live_keys[:, None, None, :], raw_scores, MASKED)

    scores = scores_of(all_keys)
    row_max = jnp.max(scores, axis=-1, keepdims=True)
    exponent = jnp.exp(scores - row_max)
    row_sum = jnp.sum(exponent, axis=-1, keepdims=True)
    soft_weights = exponent / row_sum
    log_total = row_max + jnp.log(row_sum)
    attended = jnp.einsum(
        "ghqk,gkhe->gqhe",
        soft_weights.astype(jnp.bfloat16),
        all_values,
        preferred_element_type=jnp.float32,
    )
    attended = attended.astype(jnp.bfloat16).reshape(group_count, shard_len, model_width)
    attn_result, out_mid = project(attended, 3, w_out)
    mixed = inputs + attn_result
    moe_normed = rms_norm(mixed, moe_gain).astype(jnp.bfloat16)
    tok_count = group_count * shard_len
    top_count = expert_ids.shape[-1]
    exp_devices = lax.axis_size("exp")
    local_experts = expert_gate.shape[0]
    experts = local_experts * exp_devices
    capacity = 3 * tok_count * top_count // (2 * experts)
    chosen = expert_ids.reshape(tok_count * top_count)
    gate_rows = gate_weights.reshape(tok_count, top_count)
    match_table = (chosen[:, None] == jnp.arange(experts, dtype=jnp.int32)[None, :]).astype(
        jnp.int32
    )
    slot_rank = jnp.sum((jnp.cumsum(match_table, axis=0) - match_table) * match_table, axis=1)
    owner_dev = chosen // local_experts
    local_idx = chosen % local_experts
    slot_index = local_idx * (exp_devices * capacity) + owner_dev * capacity + slot_rank
    buffer_rows = local_experts * exp_devices * capacity

    def dispatch_rows(row_block):
        filled = jnp.zeros((buffer_rows, model_width), jnp.bfloat16).at[slot_index].set(row_block)
        return filled.reshape(local_experts, exp_devices, capacity, model_width)

    def collect_rows(arrived):
        return arrived.reshape(buffer_rows, model_width)[slot_index].reshape(
            tok_count, top_count, model_width
        )

    sending = dispatch_rows(
        jnp.repeat(moe_normed.reshape(tok_count, model_width), top_count, axis=0)
    )
    received = lax.all_to_all(sending, "exp", split_axis=1, concat_axis=1, tiled=True).reshape(
        local_experts, exp_devices * capacity, model_width
    )
    gate_act = jnp.einsum("ecd,edf->ecf", received, expert_gate, preferred_element_type=jnp.float32)
    up_act = jnp.einsum("ecd,edf->ecf", received, expert_up, preferred_element_type=jnp.float32)
    hidden = (silu_value(gate_act) * up_act).astype(jnp.bfloat16)
    produced = jnp.einsum(
        "ecf,efd->ecd", hidden, expert_down, preferred_element_type=jnp.float32
    ).astype(jnp.bfloat16)
    produced = produced.reshape(local_experts, exp_devices, capacity, model_width)
    returned = collect_rows(
        lax.all_to_all(produced, "exp", split_axis=1, concat_axis=1, tiled=True)
    )
    combined = jnp.sum(gate_rows[:, :, None] * returned.astype(jnp.float32), axis=1)
    output = mixed + combined.reshape(group_count, shard_len, model_width)
    upstream = cotangent.astype(jnp.float32) * live_rows[:, :, None]
    slot_grad = (gate_rows[:, :, None] * upstream.reshape(tok_count, 1, model_width)).astype(
        jnp.bfloat16
    )
    grad_sending = dispatch_rows(slot_grad.reshape(tok_count * top_count, model_width))
    grad_arrived = lax.all_to_all(
        grad_sending, "exp", split_axis=1, concat_axis=1, tiled=True
    ).reshape(local_experts, exp_devices * capacity, model_width)
    grad_hidden = jnp.einsum(
        "ecd,efd->ecf", grad_arrived, expert_down, preferred_element_type=jnp.float32
    )
    grad_gate = (grad_hidden * up_act * silu_slope(gate_act)).astype(jnp.bfloat16)
    grad_up_act = (grad_hidden * silu_value(gate_act)).astype(jnp.bfloat16)
    grad_row = jnp.einsum(
        "ecf,edf->ecd", grad_gate, expert_gate, preferred_element_type=jnp.float32
    )
    grad_row = grad_row + jnp.einsum(
        "ecf,edf->ecd", grad_up_act, expert_up, preferred_element_type=jnp.float32
    )
    grad_row = grad_row.astype(jnp.bfloat16).reshape(
        local_experts, exp_devices, capacity, model_width
    )
    grad_back = collect_rows(
        lax.all_to_all(grad_row, "exp", split_axis=1, concat_axis=1, tiled=True)
    )
    grad_moe = jnp.sum(grad_back.astype(jnp.float32), axis=1).reshape(
        group_count, shard_len, model_width
    )
    grad_mixed = upstream + norm_back(mixed, moe_gain, grad_moe)
    grad_attended, down_out, up_out = project_back(
        grad_mixed.astype(jnp.bfloat16), attended, out_mid, 3, w_out
    )
    grad_heads = grad_attended.astype(jnp.bfloat16).reshape(
        group_count, shard_len, head_count, HEAD
    )
    key_source, value_source = (all_keys, all_values)
    probs_again = jnp.exp(scores_of(key_source) - log_total)
    grad_probs = jnp.einsum(
        "gqhe,gkhe->ghqk", grad_heads, value_source, preferred_element_type=jnp.float32
    )
    inner = jnp.sum(probs_again * grad_probs, axis=-1, keepdims=True)
    grad_scores = (probs_again * (grad_probs - inner)).astype(jnp.bfloat16)
    grad_queries = (
        jnp.einsum("ghqk,gkhe->gqhe", grad_scores, key_source, preferred_element_type=jnp.float32)
        * score_scale
    )
    grad_keys_part = (
        jnp.einsum("ghqk,gqhe->gkhe", grad_scores, queries, preferred_element_type=jnp.float32)
        * score_scale
    )
    grad_values_part = jnp.einsum(
        "ghqk,gqhe->gkhe",
        probs_again.astype(jnp.bfloat16),
        grad_heads,
        preferred_element_type=jnp.float32,
    )
    grad_keys, grad_values = (
        lax.psum_scatter(
            grad_keys_part.astype(jnp.bfloat16), "seq", scatter_dimension=1, tiled=True
        ).astype(jnp.float32),
        lax.psum_scatter(
            grad_values_part.astype(jnp.bfloat16), "seq", scatter_dimension=1, tiled=True
        ).astype(jnp.float32),
    )
    grad_query_raw = norm_back(
        query_heads, query_gain, rotate_back(grad_queries, cosine_table, sine_table)
    )
    grad_key_raw = norm_back(key_heads, key_gain, rotate_back(grad_keys, cosine_table, sine_table))
    grad_query_raw = grad_query_raw.astype(jnp.bfloat16).reshape(
        group_count, shard_len, model_width
    )
    grad_key_raw = grad_key_raw.astype(jnp.bfloat16).reshape(group_count, shard_len, model_width)
    grad_value_raw = grad_values.astype(jnp.bfloat16).reshape(group_count, shard_len, model_width)
    grad_from_query, down_query, up_query = project_back(
        grad_query_raw, normed, query_mid, 0, w_qkv[0]
    )
    grad_from_key, down_key, up_key = project_back(grad_key_raw, normed, key_mid, 1, w_qkv[1])
    grad_from_value, down_value, up_value = project_back(
        grad_value_raw, normed, value_mid, 2, w_qkv[2]
    )
    grad_normed = grad_from_query + grad_from_key + grad_from_value
    grad_input = grad_mixed + norm_back(inputs, attn_gain, grad_normed)
    per_down = jnp.stack([down_query, down_key, down_value, down_out], axis=1)
    per_up = jnp.stack([up_query, up_key, up_value, up_out], axis=1)
    choice_float = adapter_choice.astype(jnp.float32)
    grad_down = jnp.sum(choice_float[:, :, None, None, None] * per_down[:, None], axis=0)
    grad_up = jnp.sum(choice_float[:, :, None, None, None] * per_up[:, None], axis=0)
    summed_down, summed_up = (
        lax.psum(grad_down.astype(jnp.bfloat16), "seq").astype(jnp.float32),
        lax.psum(grad_up.astype(jnp.bfloat16), "seq").astype(jnp.float32),
    )
    shard_down, shard_up = (
        lax.psum_scatter(
            summed_down.astype(jnp.bfloat16), "exp", scatter_dimension=2, tiled=True
        ).astype(jnp.float32),
        lax.psum_scatter(
            summed_up.astype(jnp.bfloat16), "exp", scatter_dimension=3, tiled=True
        ).astype(jnp.float32),
    )
    new_first_down, new_second_down, new_down = adam_update(
        adapt_down, shard_down, first_down, second_down, RATE_DOWN
    )
    new_first_up, new_second_up, new_up = adam_update(
        adapt_up, shard_up, first_up, second_up, RATE_UP
    )
    return (
        output.astype(jnp.bfloat16),
        grad_input,
        new_first_down,
        new_second_down,
        new_down,
        new_first_up,
        new_second_up,
        new_up,
    )


def solution(mesh):
    in_specs = (
        P("exp", "seq", None),
        P("exp", "seq", None),
        P("exp"),
        P("exp", None),
        P("exp", "seq", None, None, None),
        P("exp", "seq", None, None, None),
        P(),
        P(),
        P(),
        P(),
        P(),
        P(),
        P("exp", None, None),
        P("exp", None, None),
        P("exp", None, None),
        P(None, None, "exp", None),
        P(None, None, "exp", None),
        P(None, None, "exp", None),
        P(None, None, None, "exp"),
        P(None, None, None, "exp"),
        P(None, None, None, "exp"),
    )
    out_specs = (
        P("exp", "seq", None),
        P("exp", "seq", None),
        P(None, None, "exp", None),
        P(None, None, "exp", None),
        P(None, None, "exp", None),
        P(None, None, None, "exp"),
        P(None, None, None, "exp"),
        P(None, None, None, "exp"),
    )
    return jax.shard_map(local, mesh=mesh, in_specs=in_specs, out_specs=out_specs, check_vma=False)
```

profile of v0, /device:TPU:0, one launch (start us, length us, event | category | flops | bytes accessed | tf_op | source)
XLA Modules:
  0.0 1309.5 jit_solution(5563968513195388759)
XLA Ops:
  27.0 14.4 %all-gather.5.cloned.1.call-done = bf16[8,4,2048,16]{2,0,3,1:T(8,128)(2,1)} async-done(((bf16[8,4,256,16]{2,0,3,1:T(8,128)(2,1)}), bf16[8,4,2048,16]{2,0,3,1:T(8,128)(2,1)}) %all-gather.5.cloned.1.call-update) | async-done | bytes 2097168 | tf_op jit(solution)/shard_map/all_gather | solution.py:124
  45.3 26.9 %all-gather.7.cloned.1.call-done = bf16[8,4,16,2048]{3,0,2,1:T(8,128)(2,1)} async-done(((bf16[8,4,16,256]{3,0,2,1:T(8,128)(2,1)}), bf16[8,4,16,2048]{3,0,2,1:T(8,128)(2,1)}) %all-gather.7.cloned.1.call-update) | async-done | bytes 2097168 | tf_op jit(solution)/shard_map/all_gather | solution.py:125
  114.2 15.9 %reduce-window.6 = s32[32,16,128]{2,1,0:T(8,128)S(1)} reduce-window(s32[32,16,128]{2,1,0:T(8,128)} %fusion.92, s32[]{:T(128)} %constant.88.clone.1), window={size=1x1x128 pad=0_0x0_0x127_0}, to_apply=%region_5.6 | reduce-window | flops 8323072 | bytes 524292 | tf_op jit(solution)/shard_map/reduce-window
  136.1 45.9 %all-gather.11.cloned.1.call-done = bf16[2,512,16,128]{3,1,2,0:T(8,128)(2,1)} async-done(((bf16[2,128,16,128]{3,1,2,0:T(8,128)(2,1)}), bf16[2,512,16,128]{3,1,2,0:T(8,128)(2,1)}) %all-gather.11.cloned.1.call-update) | async-done | bytes 4194320 | tf_op jit(solution)/shard_map/all_gather | solution.py:188
  190.9 72.2 %all-gather.9.cloned.1.call-done = bf16[2,512,16,128]{1,3,2,0:T(8,128)(2,1)} async-done(((bf16[2,128,16,128]{1,3,2,0:T(8,128)(2,1)}), bf16[2,512,16,128]{1,3,2,0:T(8,128)(2,1)}) %all-gather.9.cloned.1.call-update) | async-done | bytes 4194320 | tf_op jit(solution)/shard_map/all_gather | solution.py:189
  279.8 19.4 %scatter_custom_fusion = bf16[3072,2048]{1,0:T(8,128)(2,1)} fusion(s32[2048]{0:T(1024)S(1)} %bitcast.302, bf16[]{:T(256)} %constant.87.clone.1, bf16[256,2048]{1,0:T(8,128)(2,1)S(1)} %bitcast.295), kind=kCustom, calls=%fused_computation.16 | custom fusion | bytes 13631490 | tf_op jit(solution)/shard_map/scatter | solution.py:234
  316.3 19.9 %scatter_custom_fusion.1 = bf16[3072,2048]{1,0:T(8,128)(2,1)} fusion(s32[2048]{0:T(1024)S(1)} %bitcast.303, f32[256,2048]{1,0:T(8,128)S(1)} %bitcast.291, f32[2048]{0:T(1024)S(1)} %mul.715, bf16[]{:T(256)} %constant.87.clone.1), kind=kCustom, calls=%fused_computation.15 | custom fusion | flops 8388608 | bytes 14688258 | tf_op jit(solution)/shard_map/scatter | solution.py:234
  347.0 107.8 %all-to-all-done = bf16[4,8,96,2048]{3,2,0,1:T(8,128)(2,1)} async-done(((bf16[4,8,96,2048]{3,2,0,1:T(8,128)(2,1)}), bf16[4,8,96,2048]{3,2,0,1:T(8,128)(2,1)}, u32[]{:S(2)}, u32[]{:S(2)}) %all-to-all-start) | async-done | bytes 12582944 | tf_op jit(solution)/shard_map/all_to_all | solution.py:245
  466.5 19.5 %fusion.141 = f32[4,768,1024]{2,1,0:T(8,128)} fusion(bf16[4,768,2048]{2,1,0:T(8,128)(2,1)S(1)} %bitcast.277, bf16[4,2048,1024]{2,1,0:T(8,128)(2,1)} %param.33), kind=kOutput, calls=%fused_computation.256 | convolution fusion | flops 12884901888 | bytes 41943040 | tf_op jit(solution)/shard_map/ecd,edf->ecf/dot_general | solution.py:248
  486.0 19.5 %fusion.142 = f32[4,768,1024]{2,1,0:T(8,128)} fusion(bf16[4,768,2048]{2,1,0:T(8,128)(2,1)S(1)} %bitcast.278, bf16[4,2048,1024]{2,1,0:T(8,128)(2,1)} %param.34), kind=kOutput, calls=%fused_computation.257 | convolution fusion | flops 12884901888 | bytes 41943040 | tf_op jit(solution)/shard_map/ecd,edf->ecf/dot_general | solution.py:249
  505.5 24.7 %convolution_convert_fusion = bf16[4,768,2048]{2,1,0:T(8,128)(2,1)} fusion(bf16[4,1024,2048]{2,1,0:T(8,128)(2,1)} %param.35, f32[4,768,1024]{2,1,0:T(8,128)} %fusion.142, f32[4,768,1024]{2,1,0:T(8,128)} %fusion.141), kind=kOutput, calls=%fused_computation.52 | convolution fusion | flops 12910067712 | bytes 54525952 | tf_op jit(solution)/shard_map/ecf,efd->ecd/dot_general | solution.py:251
  540.9 58.4 %all-to-all-done.2 = bf16[4,8,96,2048]{3,2,0,1:T(8,128)(2,1)} async-done(((bf16[4,8,96,2048]{3,2,0,1:T(8,128)(2,1)}), bf16[4,8,96,2048]{3,2,0,1:T(8,128)(2,1)}, u32[]{:S(2)}, u32[]{:S(2)}) %all-to-all-start.2) | async-done | bytes 12582944 | tf_op jit(solution)/shard_map/all_to_all | solution.py:265
  615.8 21.3 %fusion.143 = f32[4,768,1024]{2,1,0:T(8,128)} fusion(bf16[4,768,2048]{2,1,0:T(8,128)(2,1)} %bitcast.279, bf16[4,1024,2048]{2,1,0:T(8,128)(2,1)} %param.35), kind=kOutput, calls=%fused_computation.258 | convolution fusion | flops 12884901888 | bytes 41943040 | tf_op jit(solution)/shard_map/ecd,efd->ecf/dot_general | solution.py:268
  637.1 28.8 %fusion.33 = f32[4,768,2048]{2,1,0:T(8,128)} fusion(bf16[4,2048,1024]{2,1,0:T(8,128)(2,1)} %param.33, f32[4,768,1024]{2,1,0:T(8,128)} %fusion.141, f32[4,768,1024]{2,1,0:T(8,128)} %fusion.143, f32[4,768,1024]{2,1,0:T(8,128)} %fusion.142), kind=kOutput, calls=%fused_computation.54 | convolution fusion | flops 12916359168 | bytes 79691776 | tf_op jit(solution)/shard_map/ecf,edf->ecd/dot_general | solution.py:273
  665.9 27.8 %add_convert_fusion = bf16[4,768,2048]{2,1,0:T(8,128)(2,1)} fusion(f32[4,768,2048]{2,1,0:T(8,128)} %fusion.33, bf16[4,2048,1024]{2,1,0:T(8,128)(2,1)} %param.34, f32[4,768,1024]{2,1,0:T(8,128)} %fusion.143, f32[4,768,1024]{2,1,0:T(8,128)} %fusion.141), kind=kOutput, calls=%fused_computation.4 | convolution fusion | flops 12916359168 | bytes 79691776 | tf_op jit(solution)/shard_map/ecf,edf->ecd/dot_general | solution.py:276
  704.5 39.6 %all-to-all-done.1 = bf16[4,8,96,2048]{3,2,0,1:T(8,128)(2,1)} async-done(((bf16[4,8,96,2048]{3,2,0,1:T(8,128)(2,1)}), bf16[4,8,96,2048]{3,2,0,1:T(8,128)(2,1)}, u32[]{:S(2)}, u32[]{:S(2)}) %all-to-all-start.1) | async-done | bytes 12582944 | tf_op jit(solution)/shard_map/all_to_all | solution.py:256
  760.6 22.5 %gather_fusion = bf16[2048,2048]{1,0:T(8,128)(2,1)} fusion(bf16[3072,2048]{1,0:T(8,128)(2,1)} %bitcast.268, s32[2048]{0:T(1024)S(1)} %broadcast_clamp_fusion), kind=kCustom, calls=%fused_computation | custom fusion | bytes 16785408 | tf_op jit(solution)/shard_map/gather | solution.py:238
  783.1 105.3 %all-to-all-done.3 = bf16[4,8,96,2048]{3,2,0,1:T(8,128)(2,1)} async-done(((bf16[4,8,96,2048]{3,2,0,1:T(8,128)(2,1)}), bf16[4,8,96,2048]{3,2,0,1:T(8,128)(2,1)}, u32[]{:S(2)}, u32[]{:S(2)}) %all-to-all-start.3) | async-done | bytes 12582944 | tf_op jit(solution)/shard_map/all_to_all | solution.py:283
  899.1 22.5 %gather_fusion.1 = bf16[2048,2048]{1,0:T(8,128)(2,1)} fusion(bf16[3072,2048]{1,0:T(8,128)(2,1)} %bitcast.267, s32[2048]{0:T(1024)S(1)} %broadcast_clamp_fusion), kind=kCustom, calls=%fused_computation.1 | custom fusion | bytes 16785408 | tf_op jit(solution)/shard_map/gather | solution.py:238
  1034.0 27.1 %reduce-scatter.13.cloned.1.call-done = bf16[128,4096]{1,0:T(8,128)(2,1)} async-done(((bf16[512,4096]{1,0:T(8,128)(2,1)}), bf16[128,4096]{1,0:T(8,128)(2,1)}) %reduce-scatter.13.cloned.1.call-update) | async-done | bytes 1048592
  1066.6 74.1 %reduce-scatter.7.cloned.1.call-done = bf16[2,128,16,128]{3,1,2,0:T(8,128)(2,1)} async-done(((bf16[2,512,16,128]{3,1,2,0:T(8,128)(2,1)}), bf16[2,128,16,128]{3,1,2,0:T(8,128)(2,1)}) %reduce-scatter.7.cloned.1.call-update) | async-done | bytes 1048592 | tf_op jit(solution)/shard_map/reduce_scatter | solution.py:317
  1199.1 13.6 %reduce-scatter.11.cloned.1.call-done = bf16[8,4,16,256]{3,2,1,0:T(8,128)(2,1)} async-done(((bf16[8,4,16,2048]{3,2,1,0:T(8,128)(2,1)}), bf16[8,4,16,256]{3,2,1,0:T(8,128)(2,1)}) %reduce-scatter.11.cloned.1.call-update) | async-done | bytes 262160 | tf_op jit(solution)/shard_map/reduce_scatter | solution.py:355
  1212.7 44.9 %reduce-scatter.9.cloned.1.call-done = bf16[8,4,256,16]{2,3,1,0:T(8,128)(2,1)} async-done(((bf16[8,4,2048,16]{2,3,1,0:T(8,128)(2,1)}), bf16[8,4,256,16]{2,3,1,0:T(8,128)(2,1)}) %reduce-scatter.9.cloned.1.call-update) | async-done | bytes 262160 | tf_op jit(solution)/shard_map/reduce_scatter | solution.py:352
  1261.1 37.5 %all-reduce.3.cloned.1.call-done = (bf16[8,4,256,16]{2,3,1,0:T(8,128)(2,1)}, bf16[8,4,16,256]{3,2,1,0:T(8,128)(2,1)}) async-done(((bf16[8,4,256,16]{2,3,1,0:T(8,128)(2,1)}, bf16[8,4,16,256]{3,2,1,0:T(8,128)(2,1)}), (bf16[8,4,256,16]{2,3,1,0:T(8,128)(2,1)}, bf16[8,4,16,256]{3,2,1,0:T(8,128)(2,1)})) %all-reduce.3.cloned.1.call-update) | async-done | bytes 524304 | tf_op jit(solution)/shard_map/psum | solution.py:348
  (371 shorter events, 384.9 us)
Async XLA Ops:
  7.2 34.2 %all-gather.5.cloned.1.call-start = ((), (), s32[]{:S(2)}) async-start(), calls=%async_computation.8 | async-start | bytes 2359296 | tf_op jit(solution)/shard_map/all_gather | solution.py:124
  9.4 62.8 %all-gather.7.cloned.1.call-start = ((), (), s32[]{:S(2)}) async-start(), calls=%async_computation.9 | async-start | bytes 2359296 | tf_op jit(solution)/shard_map/all_gather | solution.py:125
  11.5 170.5 %all-gather.11.cloned.1.call-start = ((), (), s32[]{:S(2)}) async-start(), calls=%async_computation.11 | async-start | bytes 5242880 | tf_op jit(solution)/shard_map/all_gather | solution.py:188
  44.8 232.3 %copy-start.36 = (bf16[2,2048,16]{1,0,2:T(2,128)(2,1)}, bf16[2,2048,16]{1,0,2:T(2,128)(2,1)S(1)}, u32[]{:S(2)}) copy-start(bf16[2,2048,16]{1,0,2:T(2,128)(2,1)S(1)} %get-tuple-element.34) | copy-start | bytes 393220
  99.4 82.6 %copy-start.14 = (bf16[2,128,16,64]{3,1,2,0:T(8,128)(2,1)}, bf16[2,128,16,64]{3,1,2,0:T(8,128)(2,1)S(1)}, u32[]{:S(2)}) copy-start(bf16[2,128,16,64]{3,1,2,0:T(8,128)(2,1)S(1)} %get-tuple-element.24) | copy-start | bytes 1572868
  99.4 82.6 %copy-start.16 = (bf16[2,128,16,64]{3,1,2,0:T(8,128)(2,1)}, bf16[2,128,16,64]{3,1,2,0:T(8,128)(2,1)S(1)}, u32[]{:S(2)}) copy-start(bf16[2,128,16,64]{3,1,2,0:T(8,128)(2,1)S(1)} %get-tuple-element.25) | copy-start | bytes 1572868
  101.1 162.0 %all-gather.9.cloned.1.call-start = ((), (), s32[]{:S(2)}) async-start(), calls=%async_computation.10 | async-start | bytes 5242880 | tf_op jit(solution)/shard_map/all_gather | solution.py:189
  135.3 127.8 %copy-start.54 = (pred[2,512]{1,0:T(4,128)(4,1)}, pred[2,512]{1,0:T(4,128)(4,1)S(1)}, u32[]{:S(2)}) copy-start(pred[2,512]{1,0:T(4,128)(4,1)S(1)} %iota_compare_fusion.2) | copy-start | bytes 3076
  136.1 180.2 %copy-start.80 = (s32[2048,1]{0,1:T(1,128)}, s32[2048,1]{0,1:T(1,128)S(1)}, u32[]{:S(2)}) copy-start(s32[2048,1]{0,1:T(1,128)S(1)} %compare_select_fusion) | copy-start | bytes 24580
  185.6 77.5 %copy-start.56 = (f32[2,16,128]{2,1,0:T(8,128)}, f32[2,16,128]{2,1,0:T(8,128)S(1)}, u32[]{:S(2)}) copy-start(f32[2,16,128]{2,1,0:T(8,128)S(1)} %get-tuple-element.52) | copy-start | bytes 49156
  190.9 80.0 %copy-start.66 = (f32[2,16,128]{2,1,0:T(8,128)}, f32[2,16,128]{2,1,0:T(8,128)S(1)}, u32[]{:S(2)}) copy-start(f32[2,16,128]{2,1,0:T(8,128)S(1)} %fusion.25) | copy-start | bytes 49156
  309.9 144.9 %all-to-all-start = ((bf16[4,8,96,2048]{3,2,0,1:T(8,128)(2,1)}), bf16[4,8,96,2048]{3,2,0,1:T(8,128)(2,1)}, u32[]{:S(2)}, u32[]{:S(2)}) async-start(bf16[4,8,96,2048]{3,2,0,1:T(8,128)(2,1)} %copy.437), calls=%async_computation | async-start | bytes 25165824 | tf_op jit(solution)/shard_map/all_to_all | solution.py:245
  454.8 144.5 %all-to-all-start.2 = ((bf16[4,8,96,2048]{3,2,0,1:T(8,128)(2,1)}), bf16[4,8,96,2048]{3,2,0,1:T(8,128)(2,1)}, u32[]{:S(2)}, u32[]{:S(2)}) async-start(bf16[4,8,96,2048]{3,2,0,1:T(8,128)(2,1)} %copy.442), calls=%async_computation.2 | async-start | bytes 25165824 | tf_op jit(solution)/shard_map/all_to_all | solution.py:265
  599.3 144.8 %all-to-all-start.1 = ((bf16[4,8,96,2048]{3,2,0,1:T(8,128)(2,1)}), bf16[4,8,96,2048]{3,2,0,1:T(8,128)(2,1)}, u32[]{:S(2)}, u32[]{:S(2)}) async-start(bf16[4,8,96,2048]{3,2,0,1:T(8,128)(2,1)} %copy.439), calls=%async_computation.1 | async-start | bytes 25165824 | tf_op jit(solution)/shard_map/all_to_all | solution.py:256
  744.1 144.3 %all-to-all-start.3 = ((bf16[4,8,96,2048]{3,2,0,1:T(8,128)(2,1)}), bf16[4,8,96,2048]{3,2,0,1:T(8,128)(2,1)}, u32[]{:S(2)}, u32[]{:S(2)}) async-start(bf16[4,8,96,2048]{3,2,0,1:T(8,128)(2,1)} %copy.444), calls=%async_computation.3 | async-start | bytes 25165824 | tf_op jit(solution)/shard_map/all_to_all | solution.py:283
  749.4 311.7 %reduce-scatter.13.cloned.1.call-start = ((), (), s32[]{:S(2)}) async-start(), calls=%async_computation.15 | async-start | bytes 5242880
  952.5 76.3 %copy-start.6 = (f32[2,128,2048]{2,1,0:T(8,128)}, f32[2,128,2048]{2,1,0:T(8,128)S(1)}, u32[]{:S(2)}) copy-start(f32[2,128,2048]{2,1,0:T(8,128)S(1)} %get-tuple-element.28) | copy-start | bytes 6291460
  987.8 152.9 %reduce-scatter.7.cloned.1.call-start = ((), (), s32[]{:S(2)}) async-start(), calls=%async_computation.12 | async-start | bytes 5242880 | tf_op jit(solution)/shard_map/reduce_scatter | solution.py:317
  1007.1 205.6 %reduce-scatter.11.cloned.1.call-start = ((), (), s32[]{:S(2)}) async-start(), calls=%async_computation.14 | async-start | bytes 2359296 | tf_op jit(solution)/shard_map/reduce_scatter | solution.py:355
  1065.5 76.6 %copy-start.18 = (bf16[2,128,16,128]{1,3,2,0:T(8,128)(2,1)}, bf16[2,128,16,128]{1,3,2,0:T(8,128)(2,1)S(1)}, u32[]{:S(2)}) copy-start(bf16[2,128,16,128]{1,3,2,0:T(8,128)(2,1)S(1)} %copy.503) | copy-start | bytes 3145732
  1065.5 76.6 %copy-start.42 = (f32[128,64]{1,0:T(8,128)S(1)}, f32[128,64]{1,0:T(8,128)}, u32[]{:S(2)}) copy-start(f32[128,64]{1,0:T(8,128)} %get-tuple-element.50) | copy-start | bytes 98308
  1065.5 76.6 %copy-start.44 = (f32[128,64]{1,0:T(8,128)S(1)}, f32[128,64]{1,0:T(8,128)}, u32[]{:S(2)}) copy-start(f32[128,64]{1,0:T(8,128)} %get-tuple-element.51) | copy-start | bytes 98308
  1170.8 86.8 %reduce-scatter.9.cloned.1.call-start = ((), (), s32[]{:S(2)}) async-start(), calls=%async_computation.13 | async-start | bytes 2359296 | tf_op jit(solution)/shard_map/reduce_scatter | solution.py:352
  1177.0 121.5 %all-reduce.3.cloned.1.call-start = ((), (), s32[]{:S(2)}) async-start(), calls=%async_computation.16 | async-start | bytes 1048576 | tf_op jit(solution)/shard_map/psum | solution.py:348
  (95 other events, 957.8 us)
Sparse Core Ops, SparseCore 0:
  10.5 30.8 all-gather.4
  43.9 28.2 all-gather.6
  101.2 80.7 all-gather.10
  183.9 79.0 all-gather.8
  987.9 73.1 reduce-scatter.12
  1063.4 77.2 reduce-scatter.6
  1170.9 41.7 reduce-scatter.10
  1216.3 41.2 reduce-scatter.8
  1260.0 38.5 all-reduce.2
where the time goes:
time: 1320 us; the launch traced here: 1310 us
  waiting for transfers between devices  668 us (51%)
  matrix products  248 us (19%)
  local copies, waits for them, and re-layouts  223 us (17%)
  other arithmetic  132 us (10%)
  starting transfers between devices  22.8 us (2%)
  between operations  15.2 us (1%)
    all_to_all x1, waiting for transfers between devices, local(): lax.all_to_all(sending, 'exp', split_axis=1, concat_axis=1, tiled=True)  108 us
    all_to_all x1, waiting for transfers between devices, local(): lax.all_to_all(grad_row, 'exp', split_axis=1, concat_axis=1, tiled=True)  105 us
    reduce_scatter x1, waiting for transfers between devices, local(): lax.psum_scatter(grad_keys_part.astype(jnp.bfloat16), 'seq', scatter_dime...  74.1 us
    all_gather x1, waiting for transfers between devices, local(): lax.all_gather(value_rows, 'seq', axis=1, tiled=True)  72.2 us
    all_to_all x1, waiting for transfers between devices, local(): lax.all_to_all(grad_sending, 'exp', split_axis=1, concat_axis=1, tiled=True)  58.4 us
    all_gather x1, waiting for transfers between devices, local(): lax.all_gather(key_rows, 'seq', axis=1, tiled=True)  45.9 us
    gather x2, local copies, waits for them, and re-layouts, collect_rows(): arrived.reshape(buffer_rows, model_width)[slot_index]  45 us
    reduce_scatter x1, waiting for transfers between devices, local(): lax.psum_scatter(summed_down.astype(jnp.bfloat16), 'exp', scatter_dimensi...  44.9 us
  transfers between devices with their start and end apart: 13, of which 13 were waited for; matrix products, arithmetic and copies ran while one was open for 29% of the time, Pallas kernels for 0%

commit v1 on v0

v1 whole, which is shorter than its diff:
```python
import functools

import jax
import jax.numpy as jnp
from jax import lax
from jax.experimental import pallas as pl
from jax.experimental.pallas import tpu as pltpu
from jax.sharding import PartitionSpec as P

HEAD = 128
STEP = 5

NORM_EPS = 1e-05
ROPE_BASE = 50000.0
ADAPTER_SCALE = 0.5
BETA_FIRST = 0.5
BETA_SECOND = 0.5
RATE_DOWN = 0.02
RATE_UP = 0.2
WEIGHT_DECAY = 0.01
ADAM_EPS = 1e-08
MASKED = -1e30
SCORE_SCALE = HEAD ** (-0.5)

F32 = jnp.float32
BF16 = jnp.bfloat16
VMEM_LIMIT = 60 * 1024 * 1024


def dot_nn(a, b):
    return lax.dot_general(a, b, (((1,), (0,)), ((), ())), preferred_element_type=F32)


def dot_nt(a, b):
    return lax.dot_general(a, b, (((1,), (1,)), ((), ())), preferred_element_type=F32)


def dot_tn(a, b):
    return lax.dot_general(a, b, (((0,), (0,)), ((), ())), preferred_element_type=F32)


def inverse_rms(values):
    return lax.rsqrt(jnp.mean(values * values, axis=-1, keepdims=True) + NORM_EPS)


def norm_back(values, gain, upstream):
    inverse = inverse_rms(values)
    scaled = upstream * gain
    return inverse * scaled - values * (inverse * inverse * inverse) * jnp.mean(
        values * scaled, axis=-1, keepdims=True
    )


def sigmoid(values):
    return 1.0 / (1.0 + jnp.exp(-values))


def adam_update(weight, gradient, first, second, step_rate):
    new_first = BETA_FIRST * first + (1.0 - BETA_FIRST) * gradient
    new_second = BETA_SECOND * second + (1.0 - BETA_SECOND) * gradient * gradient
    first_hat = new_first / (1.0 - BETA_FIRST**STEP)
    second_hat = new_second / (1.0 - BETA_SECOND**STEP)
    new_weight = weight - step_rate * (
        first_hat / (jnp.sqrt(second_hat) + ADAM_EPS) + WEIGHT_DECAY * weight
    )
    return (new_first, new_second, new_weight)


def shape_of(shape, dtype):
    return jax.ShapeDtypeStruct(shape, dtype)


def whole_block(shape):
    rank = len(shape)
    return pl.BlockSpec(tuple(shape), lambda *_: (0,) * rank)


def kernel_call(
    body, name, grid, in_specs, out_specs, out_shape, scratch=(), prefetch=0, flops=0, moved=0
):
    return pl.pallas_call(
        body,
        grid_spec=pltpu.PrefetchScalarGridSpec(
            num_scalar_prefetch=prefetch,
            grid=grid,
            in_specs=in_specs,
            out_specs=out_specs,
            scratch_shapes=list(scratch),
        ),
        out_shape=out_shape,
        name=name,
        cost_estimate=pl.CostEstimate(
            flops=int(flops), bytes_accessed=int(moved), transcendentals=0
        ),
        compiler_params=pltpu.CompilerParams(vmem_limit_bytes=VMEM_LIMIT),
    )


def swap(values, mask):
    count = lax.axis_size("exp")
    return lax.ppermute(values, "exp", [(i, i ^ mask) for i in range(count)])


def by_relative(stacked):
    count = lax.axis_size("exp")
    return jnp.take(stacked, lax.axis_index("exp") ^ jnp.arange(count), axis=0)


def gather_rows(rows):
    count = lax.axis_size("exp")
    if count != 8:
        everything = by_relative(lax.all_gather(rows, "exp"))
        return [(m, 0, everything[m]) for m in range(count)]
    half = rows.shape[0] // 2
    by_x = swap(rows, 2)
    by_y = swap(rows, 4)
    far_front = swap(by_x[:half], 4)
    far_back = swap(by_y[half:], 2)
    pieces = [(0, 0, rows), (2, 0, by_x), (4, 0, by_y), (6, 0, far_front), (6, half, far_back)]
    return pieces + [(m + 1, first, swap(array, 1)) for m, first, array in pieces]


def stack_pieces(pieces):
    count = lax.axis_size("exp")
    ordered = []
    for m in range(count):
        own = sorted(
            [(first, index) for index, (at, first, _) in enumerate(pieces) if at == m]
        )
        ordered.append(jnp.concatenate([pieces[index][2] for _, index in own], axis=0))
    return jnp.stack(ordered)


def add_low(a, b):
    return (a.astype(F32) + b.astype(F32)).astype(BF16)


def scatter_sum(parts):
    count = lax.axis_size("exp")
    if count != 8:
        sent = by_relative(jnp.stack(parts))
        came = lax.all_to_all(sent, "exp", 0, 0)
        return [(0, came[i]) for i in range(count)]
    half = parts[0].shape[0] // 2
    paired = {m: add_low(parts[m], swap(parts[m + 1], 1)) for m in (6, 4, 2)}
    beside = swap(parts[1], 1)
    far_front = swap(paired[6][:half], 2)
    far_back = swap(paired[6][half:], 4)
    x_front = swap(paired[2][:half], 2)
    y_back = swap(paired[4][half:], 4)
    y_front = swap(add_low(paired[4][:half], far_front), 4)
    x_back = swap(add_low(paired[2][half:], far_back), 2)
    return [
        (0, parts[0]),
        (0, beside),
        (0, x_front),
        (half, y_back),
        (0, y_front),
        (half, x_back),
    ]


def project_first(tokens, gain, w_qkv, groups, splits):
    rows, width = tokens.shape
    part = width // splits
    shard = rows // groups

    def body(tok_ref, gain_ref, w_ref, *outs):
        normed_ref = outs[groups]

        @pl.when((pl.program_id(0) == 0) & (pl.program_id(1) == 0))
        def _():
            values = tok_ref[...].astype(F32)
            normed_ref[...] = (values * inverse_rms(values) * gain_ref[...]).astype(BF16)

        result = dot_nn(normed_ref[...], w_ref[0])
        for g in range(groups):
            outs[g][0, 0] = result[g * shard : (g + 1) * shard].astype(BF16)

    return kernel_call(
        body,
        "project_first",
        (3, splits),
        [
            whole_block((rows, width)),
            whole_block((1, width)),
            pl.BlockSpec((1, width, part), lambda p, j: (p, 0, j)),
        ],
        [pl.BlockSpec((1, 1, shard, part), lambda p, j: (j, p, 0, 0))] * groups
        + [whole_block((rows, width))],
        [shape_of((splits, 3, shard, part), BF16)] * groups + [shape_of((rows, width), BF16)],
        flops=6 * rows * width * width,
        moved=6 * width * width,
    )(tokens, gain, w_qkv)


def pick_sets(stacked, picks, groups):
    count, kinds, _, projections, rank, part = stacked.shape

    def body(pick_ref, in_ref, out_ref):
        out_ref[0] = in_ref[0, :, 0]

    return kernel_call(
        body,
        "pick_sets",
        (groups, count),
        [
            pl.BlockSpec(
                (1, kinds, 1, projections, rank, part),
                lambda g, j, s: (j ^ s[groups], 0, s[g], 0, 0, 0),
            )
        ],
        pl.BlockSpec((1, kinds, projections, rank, part), lambda g, j, s: (g, 0, 0, 0, j)),
        shape_of((groups, kinds, projections, rank, count * part), BF16),
        prefetch=1,
        moved=8 * groups * count * projections * rank * part,
    )(picks, stacked)


def wide_mids(mids, which, rank):
    splits = mids.shape[0]
    return jnp.concatenate(
        [mids[z, which * rank : (which + 1) * rank, :] for z in range(splits)], axis=1
    )


def rotate(values, cosine, sine):
    return values * cosine + pltpu.roll(values, HEAD // 2, 1) * sine


def rotate_back(values, cosine, sine):
    return values * cosine - pltpu.roll(values, HEAD // 2, 1) * sine


def softmax_rows(queries, keys, length):
    total = keys.shape[0]
    scores = dot_nt(queries, keys) * SCORE_SCALE
    live = lax.broadcasted_iota(jnp.int32, (1, total), 1) < length
    scores = jnp.where(live, scores, MASKED)
    exponent = jnp.exp(scores - jnp.max(scores, axis=-1, keepdims=True))
    return exponent / jnp.sum(exponent, axis=-1, keepdims=True)


def attend(length, raw, mids, ups, query_gain, key_gain, cosine, sine):
    splits, _, shard, part = raw.shape
    rank = ups.shape[1]
    total = splits * shard
    heads = part // HEAD

    def body(
        len_ref, raw_ref, mid_ref, up_ref, qg_ref, kg_ref, cos_ref, sin_ref,
        att_ref, q_ref, k_ref, v_ref, rq_ref, rk_ref,
    ):
        mid = mid_ref[...]

        def full(which):
            base = raw_ref[:, which].reshape(total, HEAD).astype(F32)
            return base + ADAPTER_SCALE * dot_tn(wide_mids(mid, which, rank), up_ref[which])

        raw_q, raw_k, raw_v = full(0), full(1), full(2)
        rq_ref[0] = raw_q
        rk_ref[0] = raw_k
        cosine, sine = cos_ref[...], sin_ref[...]
        queries = rotate(raw_q * inverse_rms(raw_q) * qg_ref[...], cosine, sine).astype(BF16)
        keys = rotate(raw_k * inverse_rms(raw_k) * kg_ref[...], cosine, sine).astype(BF16)
        values = raw_v.astype(BF16)
        q_ref[0] = queries
        k_ref[0] = keys
        v_ref[0] = values
        weights = softmax_rows(queries, keys, len_ref[0]).astype(BF16)
        att_ref[...] = dot_nn(weights, values).astype(BF16).reshape(splits, shard, HEAD)

    head_block = pl.BlockSpec((1, total, HEAD), lambda h, s: (h, 0, 0))
    return kernel_call(
        body,
        "attend",
        (heads,),
        [
            pl.BlockSpec((splits, 3, shard, HEAD), lambda h, s: (0, 0, 0, h)),
            whole_block(mids.shape),
            pl.BlockSpec((3, rank, HEAD), lambda h, s: (0, 0, h)),
            whole_block((1, HEAD)),
            whole_block((1, HEAD)),
            whole_block((total, HEAD)),
            whole_block((total, HEAD)),
        ],
        [pl.BlockSpec((splits, shard, HEAD), lambda h, s: (0, 0, h))] + [head_block] * 5,
        [shape_of((splits, shard, part), BF16)]
        + [shape_of((heads, total, HEAD), BF16)] * 3
        + [shape_of((heads, total, HEAD), F32)] * 2,
        prefetch=1,
        flops=4 * heads * total * total * HEAD,
        moved=heads * total * HEAD * 24 + 4 * heads * total * total,
    )(length, raw, mids, ups, query_gain, key_gain, cosine, sine)


def attend_back(length, grads, q, k, v, raw_q, raw_k, query_gain, key_gain, cosine, sine):
    splits, shard, part = grads.shape
    total = splits * shard
    heads = part // HEAD

    def body(
        len_ref, grad_ref, q_ref, k_ref, v_ref, rq_ref, rk_ref, qg_ref, kg_ref, cos_ref, sin_ref,
        out_ref,
    ):
        queries, keys, values = q_ref[0], k_ref[0], v_ref[0]
        grad = grad_ref[...].reshape(total, HEAD)
        weights = softmax_rows(queries, keys, len_ref[0])
        grad_probs = dot_nt(grad, values)
        inner = jnp.sum(weights * grad_probs, axis=-1, keepdims=True)
        grad_scores = (weights * (grad_probs - inner)).astype(BF16)
        grad_q = dot_nn(grad_scores, keys) * SCORE_SCALE
        grad_k = dot_tn(grad_scores, queries) * SCORE_SCALE
        grad_v = dot_tn(weights.astype(BF16), grad)
        cosine, sine = cos_ref[...], sin_ref[...]
        grad_q = norm_back(rq_ref[0], qg_ref[...], rotate_back(grad_q, cosine, sine))
        grad_k = norm_back(rk_ref[0], kg_ref[...], rotate_back(grad_k, cosine, sine))
        for which, value in enumerate((grad_q, grad_k, grad_v)):
            out_ref[:, which] = value.astype(BF16).reshape(splits, shard, HEAD)

    head_block = pl.BlockSpec((1, total, HEAD), lambda h, s: (h, 0, 0))
    return kernel_call(
        body,
        "attend_back",
        (heads,),
        [pl.BlockSpec((splits, shard, HEAD), lambda h, s: (0, 0, h))]
        + [head_block] * 5
        + [
            whole_block((1, HEAD)),
            whole_block((1, HEAD)),
            whole_block((total, HEAD)),
            whole_block((total, HEAD)),
        ],
        pl.BlockSpec((splits, 3, shard, HEAD), lambda h, s: (0, 0, 0, h)),
        shape_of((splits, 3, shard, part), BF16),
        prefetch=1,
        flops=10 * heads * total * total * HEAD,
        moved=heads * total * HEAD * 24 + 8 * heads * total * total,
    )(length, grads, q, k, v, raw_q, raw_k, query_gain, key_gain, cosine, sine)


def project_out(attended, w_out, down, up, tokens, gain):
    splits, shard, part = attended.shape
    width = splits * part
    rank = down.shape[0]
    block = min(512, width)
    steps = width // block

    def body(att_ref, w_ref, down_ref, up_ref, tok_ref, gain_ref, mixed_ref, moe_ref, mid_ref, att):
        step = pl.program_id(0)

        @pl.when(step == 0)
        def _():
            for z in range(splits):
                att[:, z * part : (z + 1) * part] = att_ref[z]
            mid_ref[...] = dot_nt(down_ref[...], att[...]).astype(BF16)

        columns = pl.ds(pl.multiple_of(step * block, block), block)
        mixed_ref[:, columns] = (
            tok_ref[:, columns].astype(F32)
            + dot_nn(att[...], w_ref[...])
            + ADAPTER_SCALE * dot_tn(mid_ref[...], up_ref[:, columns])
        )

        @pl.when(step == steps - 1)
        def _():
            values = mixed_ref[...]
            moe_ref[...] = (values * inverse_rms(values) * gain_ref[...]).astype(BF16)

    return kernel_call(
        body,
        "project_out",
        (steps,),
        [
            whole_block(attended.shape),
            pl.BlockSpec((width, block), lambda i: (0, i)),
            whole_block((rank, width)),
            whole_block((rank, width)),
            whole_block((shard, width)),
            whole_block((1, width)),
        ],
        [whole_block((shard, width)), whole_block((shard, width)), whole_block((rank, shard))],
        [
            shape_of((shard, width), F32),
            shape_of((shard, width), BF16),
            shape_of((rank, shard), BF16),
        ],
        scratch=[pltpu.VMEM((shard, width), BF16)],
        flops=2 * shard * width * width,
        moved=2 * width * width,
    )(attended, w_out, down, up, tokens, gain)


def one_hot(slot_row, capacity):
    tokens = slot_row.shape[1]
    index = lax.broadcasted_iota(jnp.int32, (capacity, tokens), 0).astype(F32)
    return index == slot_row


def load_pieces(pieces, refs, target, sem, shard):
    copies = []
    for index, (ref, (g, m, first, count)) in enumerate(zip(refs, pieces)):
        copies.append(
            pltpu.make_async_copy(
                ref, target.at[m, pl.ds(g * shard + first, count)], sem.at[index]
            )
        )
    for copy in copies:
        copy.start()
    for copy in copies:
        copy.wait()


def piece_list(gathered):
    places, arrays = [], []
    for g, pieces in enumerate(gathered):
        for m, first, array in pieces:
            places.append((g, m, first, array.shape[0]))
            arrays.append(array)
    return places, arrays


def expert_grad_hidden(gathered, meta, expert_down, capacity):
    places, arrays = piece_list(gathered)
    shard = sum(place[3] for place in places if place[:2] == (0, 0))
    experts, hidden, width = expert_down.shape
    count = meta.shape[0]
    tokens = meta.shape[-1]
    rows = count * capacity

    def body(meta_ref, w_ref, *rest):
        refs, (out_ref, held, picked, sem) = rest[: len(arrays)], rest[len(arrays) :]
        expert = pl.program_id(0)

        @pl.when(expert == 0)
        def _():
            load_pieces(places, refs, held, sem, shard)

        for m in range(count):
            named = one_hot(meta_ref[m, 0, pl.ds(expert, 1)], capacity)
            weight = jnp.sum(
                jnp.where(named, meta_ref[m, 1, pl.ds(expert, 1)], 0.0), axis=1, keepdims=True
            )
            picked[m * capacity : (m + 1) * capacity] = (
                weight * dot_nn(named.astype(BF16), held[m])
            ).astype(BF16)
        out_ref[0] = dot_nt(picked[...], w_ref[0]).astype(BF16)

    return kernel_call(
        body,
        "expert_grad_hidden",
        (experts,),
        [
            whole_block(meta.shape),
            pl.BlockSpec((1, hidden, width), lambda e: (e, 0, 0)),
        ]
        + [pl.BlockSpec(memory_space=pl.ANY)] * len(arrays),
        pl.BlockSpec((1, rows, hidden), lambda e: (e, 0, 0)),
        shape_of((experts, rows, hidden), BF16),
        scratch=[
            pltpu.VMEM((count, tokens, width), BF16),
            pltpu.VMEM((rows, width), BF16),
            pltpu.SemaphoreType.DMA((len(arrays),)),
        ],
        flops=2 * experts * rows * (hidden + tokens) * width,
        moved=2 * experts * hidden * width + 2 * count * tokens * width,
    )(meta, expert_down, *arrays)


def expert_middle(gathered, meta, expert_gate, expert_up, grad_hidden, capacity):
    places, arrays = piece_list(gathered)
    shard = sum(place[3] for place in places if place[:2] == (0, 0))
    experts, width, hidden = expert_gate.shape
    count = meta.shape[0]
    tokens = meta.shape[-1]
    rows = count * capacity
    block = min(512, hidden)
    steps = hidden // block
    chunk = 256 if rows % 256 == 0 else rows

    def body(meta_ref, gate_ref, up_ref, gh_ref, *rest):
        refs, (h_ref, gx_ref, held, picked, total, sem) = rest[: len(arrays)], rest[len(arrays) :]
        expert, step = pl.program_id(0), pl.program_id(1)

        @pl.when((expert == 0) & (step == 0))
        def _():
            load_pieces(places, refs, held, sem, shard)

        @pl.when(step == 0)
        def _():
            for m in range(count):
                named = one_hot(meta_ref[m, 0, pl.ds(expert, 1)], capacity)
                picked[m * capacity : (m + 1) * capacity] = dot_nn(
                    named.astype(BF16), held[m]
                ).astype(BF16)

        for c in range(rows // chunk):
            at = slice(c * chunk, (c + 1) * chunk)
            x = picked[at]
            gate = dot_nn(x, gate_ref[0])
            up = dot_nn(x, up_ref[0])
            sigma = sigmoid(gate)
            value = gate * sigma
            grad = gh_ref[0, at].astype(F32)
            h_ref[0, at] = (value * up).astype(BF16)
            grad_gate = (grad * up * (sigma * (1.0 + gate * (1.0 - sigma)))).astype(BF16)
            grad_up = (grad * value).astype(BF16)
            grad_x = dot_nt(grad_gate, gate_ref[0]) + dot_nt(grad_up, up_ref[0])

            @pl.when(step == 0)
            def _():
                total[at] = grad_x

            @pl.when((step > 0) & (step < steps - 1))
            def _():
                total[at] += grad_x

            @pl.when(step == steps - 1)
            def _():
                gx_ref[0, at] = (total[at] + grad_x).astype(BF16)

    return kernel_call(
        body,
        "expert_middle",
        (experts, steps),
        [
            whole_block(meta.shape),
            pl.BlockSpec((1, width, block), lambda e, f: (e, 0, f)),
            pl.BlockSpec((1, width, block), lambda e, f: (e, 0, f)),
            pl.BlockSpec((1, rows, block), lambda e, f: (e, 0, f)),
        ]
        + [pl.BlockSpec(memory_space=pl.ANY)] * len(arrays),
        [
            pl.BlockSpec((1, rows, block), lambda e, f: (e, 0, f)),
            pl.BlockSpec((1, rows, width), lambda e, f: (e, 0, 0)),
        ],
        [shape_of((experts, rows, hidden), BF16), shape_of((experts, rows, width), BF16)],
        scratch=[
            pltpu.VMEM((count, tokens, width), BF16),
            pltpu.VMEM((rows, width), BF16),
            pltpu.VMEM((rows, width), F32),
            pltpu.SemaphoreType.DMA((len(arrays),)),
        ],
        flops=2 * experts * rows * (4 * hidden + tokens) * width,
        moved=4 * experts * hidden * width + 4 * experts * rows * width,
    )(meta, expert_gate, expert_up, grad_hidden, *arrays)


def expert_produce(hidden_rows, meta, expert_down, capacity):
    experts, hidden, width = expert_down.shape
    count = meta.shape[0]
    rows = count * capacity

    def body(meta_ref, h_ref, w_ref, out_ref):
        expert = pl.program_id(0)
        result = dot_nn(h_ref[0], w_ref[0])
        for m in range(count):
            named = one_hot(meta_ref[m, 0, pl.ds(expert, 1)], capacity)
            weight = jnp.sum(
                jnp.where(named, meta_ref[m, 1, pl.ds(expert, 1)], 0.0), axis=1, keepdims=True
            )
            at = slice(m * capacity, (m + 1) * capacity)
            out_ref[0, at] = (weight * result[at]).astype(BF16)

    return kernel_call(
        body,
        "expert_produce",
        (experts,),
        [
            whole_block(meta.shape),
            pl.BlockSpec((1, rows, hidden), lambda e: (e, 0, 0)),
            pl.BlockSpec((1, hidden, width), lambda e: (e, 0, 0)),
        ],
        pl.BlockSpec((1, rows, width), lambda e: (e, 0, 0)),
        shape_of((experts, rows, width), BF16),
        flops=2 * experts * rows * hidden * width,
        moved=2 * experts * hidden * width + 2 * experts * rows * width,
    )(meta, hidden_rows, expert_down)


def combine(slot_rows, meta, members, capacity, groups):
    experts, rows, width = slot_rows.shape
    tokens = meta.shape[-1]
    shard = tokens // groups
    block = min(512, width)
    size = len(members)
    start = members[0]
    depth = experts * capacity

    def body(meta_ref, in_ref, *rest):
        outs, named = rest[:-1], rest[-1]

        @pl.when(pl.program_id(0) == 0)
        def _():
            for i, m in enumerate(members):
                for e in range(experts):
                    named[i, e * capacity : (e + 1) * capacity] = one_hot(
                        meta_ref[m, 0, e : e + 1], capacity
                    ).astype(BF16)

        for i in range(size):
            held = in_ref[:, i * capacity : (i + 1) * capacity].reshape(depth, block)
            result = dot_tn(named[i], held).astype(BF16)
            for g in range(groups):
                outs[i * groups + g][...] = result[g * shard : (g + 1) * shard]

    result = kernel_call(
        body,
        "combine",
        (width // block,),
        [
            whole_block(meta.shape),
            pl.BlockSpec((experts, size * capacity, block), lambda c: (0, start // size, c)),
        ],
        [pl.BlockSpec((shard, block), lambda c: (0, c))] * (size * groups),
        [shape_of((shard, width), BF16)] * (size * groups),
        scratch=[pltpu.VMEM((size, depth, tokens), BF16)],
        flops=2 * size * depth * tokens * width,
        moved=2 * size * (depth + tokens) * width,
    )(meta, slot_rows)
    return [result[i * groups : (i + 1) * groups] for i in range(size)]


def combine_all(slot_rows, meta, capacity, groups):
    count = meta.shape[0]
    parts = {}
    for start in reversed(range(0, count, 2)):
        for m, part in zip(
            (start, start + 1), combine(slot_rows, meta, (start, start + 1), capacity, groups)
        ):
            parts[m] = part
    return [[parts[m][g] for m in range(count)] for g in range(groups)]


def project_out_back(pieces, mixed, upstream, gain, w_out, down, up, attended, mid):
    splits, shard, part = attended.shape
    width = splits * part
    rank = down.shape[0]
    places = [(first, array.shape[0]) for first, array in pieces]

    def body(mixed_ref, up_stream_ref, gain_ref, w_ref, down_ref, up_ref, att_ref, mid_ref, *rest):
        refs = rest[: len(places)]
        gm_ref, out_ref, gdown_ref, gup_ref, low, small = rest[len(places) :]
        step = pl.program_id(0)

        @pl.when(step == 0)
        def _():
            gm_ref[...] = jnp.zeros((shard, width), F32)
            for ref, (first, count) in zip(refs, places):
                gm_ref[first : first + count] += ref[...].astype(F32)
            grad = up_stream_ref[...].astype(F32) + norm_back(
                mixed_ref[...], gain_ref[...], gm_ref[...]
            )
            gm_ref[...] = grad
            low[...] = grad.astype(BF16)
            small[...] = (ADAPTER_SCALE * dot_nt(up_ref[...], low[...])).astype(BF16)
            gup_ref[...] = (ADAPTER_SCALE * dot_nn(mid_ref[...], low[...])).astype(BF16)

        columns = pl.ds(pl.multiple_of(step * part, part), part)
        out_ref[0] = (
            dot_nt(low[...], w_ref[...]) + dot_tn(small[...], down_ref[:, columns])
        ).astype(BF16)
        gdown_ref[...] = dot_nn(small[...], att_ref[0]).astype(BF16)

    return kernel_call(
        body,
        "project_out_back",
        (splits,),
        [
            whole_block((shard, width)),
            whole_block((shard, width)),
            whole_block((1, width)),
            pl.BlockSpec((part, width), lambda j: (j, 0)),
            whole_block((rank, width)),
            whole_block((rank, width)),
            pl.BlockSpec((1, shard, part), lambda j: (j, 0, 0)),
            whole_block((rank, shard)),
        ]
        + [whole_block((count, width)) for _, count in places],
        [
            whole_block((shard, width)),
            pl.BlockSpec((1, shard, part), lambda j: (j, 0, 0)),
            pl.BlockSpec((rank, part), lambda j: (0, j)),
            whole_block((rank, width)),
        ],
        [
            shape_of((shard, width), F32),
            shape_of((splits, shard, part), BF16),
            shape_of((rank, width), BF16),
            shape_of((rank, width), BF16),
        ],
        scratch=[pltpu.VMEM((shard, width), BF16), pltpu.VMEM((rank, shard), BF16)],
        flops=2 * shard * width * width,
        moved=2 * width * width,
    )(mixed, upstream, gain, w_out, down, up, attended, mid, *[array for _, array in pieces])


def adapter_grads(grads, normed, mids, downs_ups):
    groups = len(grads)
    splits, _, shard, part = grads[0].shape
    width = splits * part
    rank = downs_ups.shape[3]

    def body(normed_ref, mid_ref, up_ref, *rest):
        refs = rest[:groups]
        small_ref, gdown_ref, gup_ref, low = rest[groups:]
        for g in range(groups):
            for z in range(splits):
                low[:, z * part : (z + 1) * part] = refs[g][z, 0]
            small = (ADAPTER_SCALE * dot_nt(up_ref[g, 0, 0], low[...])).astype(BF16)
            small_ref[g, 0] = small
            gdown_ref[g, 0] = dot_nn(small, normed_ref[g * shard : (g + 1) * shard]).astype(BF16)
            gup_ref[g, 0] = (ADAPTER_SCALE * dot_nn(mid_ref[g, 0], low[...])).astype(BF16)

    wide = pl.BlockSpec((groups, 1, rank, width), lambda p: (0, p, 0, 0))
    return kernel_call(
        body,
        "adapter_grads",
        (3,),
        [
            whole_block(normed.shape),
            pl.BlockSpec((groups, 1, rank, shard), lambda p: (0, p, 0, 0)),
            pl.BlockSpec((groups, 1, 1, rank, width), lambda p: (0, 1, p, 0, 0)),
        ]
        + [pl.BlockSpec((splits, 1, shard, part), lambda p: (0, p, 0, 0))] * groups,
        [pl.BlockSpec((groups, 1, rank, shard), lambda p: (0, p, 0, 0)), wide, wide],
        [
            shape_of((groups, 3, rank, shard), BF16),
            shape_of((groups, 3, rank, width), BF16),
            shape_of((groups, 3, rank, width), BF16),
        ],
        scratch=[pltpu.VMEM((shard, width), BF16)],
        flops=18 * groups * shard * rank * width,
        moved=6 * groups * shard * width,
    )(normed, mids, downs_ups, *grads)


def project_first_back(grads, smalls, downs_ups, w_qkv, tokens, gain, grad_mixed):
    groups = len(grads)
    splits, _, shard, part = grads[0].shape
    width = splits * part
    rank = downs_ups.shape[3]
    rows = groups * shard
    block = min(512, width)
    steps = width // block

    def body(small_ref, down_ref, w_ref, tok_ref, gain_ref, *rest):
        mixed_refs, refs = rest[:groups], rest[groups : 2 * groups]
        out_ref, low, total = rest[2 * groups :]
        which, step = pl.program_id(0), pl.program_id(1)

        @pl.when(step == 0)
        def _():
            for g in range(groups):
                for z in range(splits):
                    low[g * shard : (g + 1) * shard, z * part : (z + 1) * part] = refs[g][z, 0]

        columns = pl.ds(pl.multiple_of(step * block, block), block)
        result = dot_nt(low[...], w_ref[0])
        small = jnp.concatenate(
            [dot_tn(small_ref[g, 0], down_ref[g, 0, 0]) for g in range(groups)], axis=0
        )

        @pl.when(which == 0)
        def _():
            total[:, columns] = result + small

        @pl.when(which > 0)
        def _():
            total[:, columns] += result + small

        @pl.when((which == 2) & (step == steps - 1))
        def _():
            back = norm_back(tok_ref[...].astype(F32), gain_ref[...], total[...])
            for g in range(groups):
                out_ref[g] = mixed_refs[g][...] + back[g * shard : (g + 1) * shard]

    return kernel_call(
        body,
        "project_first_back",
        (3, steps),
        [
            pl.BlockSpec((groups, 1, rank, shard), lambda p, i: (0, p, 0, 0)),
            pl.BlockSpec((groups, 1, 1, rank, block), lambda p, i: (0, 0, p, 0, i)),
            pl.BlockSpec((1, block, width), lambda p, i: (p, i, 0)),
            whole_block((rows, width)),
            whole_block((1, width)),
        ]
        + [whole_block((shard, width))] * groups
        + [pl.BlockSpec((splits, 1, shard, part), lambda p, i: (0, p, 0, 0))] * groups,
        whole_block((groups, shard, width)),
        shape_of((groups, shard, width), F32),
        scratch=[pltpu.VMEM((rows, width), BF16), pltpu.VMEM((rows, width), F32)],
        flops=6 * rows * width * width,
        moved=6 * width * width,
    )(smalls, downs_ups, w_qkv, tokens, gain, *grad_mixed, *grads)


def local(
    tokens,
    cotangent,
    lengths,
    adapter_choice,
    expert_ids,
    gate_weights,
    attn_gain,
    moe_gain,
    query_gain,
    key_gain,
    w_qkv,
    w_out,
    expert_gate,
    expert_up,
    expert_down,
    adapt_down,
    first_down,
    second_down,
    adapt_up,
    first_up,
    second_up,
):
    groups, shard, width = tokens.shape
    splits = lax.axis_size("seq")
    devices = lax.axis_size("exp")
    here = lax.axis_index("seq")
    total = shard * splits
    part = width // splits
    rows = groups * shard
    sets, projections, slice_width, rank = adapt_down.shape
    local_experts = expert_gate.shape[0]
    experts = local_experts * devices
    top = expert_ids.shape[-1]
    capacity = 3 * rows * top // (2 * experts)

    flat_tokens = tokens.reshape(rows, width)
    gain_row = attn_gain.reshape(1, width)
    moe_row = moe_gain.reshape(1, width)
    query_row = query_gain.reshape(1, HEAD)
    key_row = key_gain.reshape(1, HEAD)

    positions = here * shard + jnp.arange(shard, dtype=jnp.int32)
    own_live = positions[None, :] < lengths[:, None]
    upstream = jnp.where(own_live[:, :, None], cotangent, jnp.zeros((), BF16))

    frequency = ROPE_BASE ** (-(2.0 / HEAD) * jnp.arange(HEAD // 2, dtype=F32))
    angles = jnp.arange(total, dtype=F32)[:, None] * frequency[None, :]
    cosine, sine = jnp.cos(angles), jnp.sin(angles)
    cosine = jnp.concatenate([cosine, cosine], axis=1)
    sine = jnp.concatenate([-sine, sine], axis=1)

    first = project_first(flat_tokens, gain_row, w_qkv, groups, splits)
    normed = first[groups]
    raw = [lax.all_to_all(first[g], "seq", 0, 0) for g in range(groups)]

    packed = jnp.stack([jnp.swapaxes(adapt_down.astype(BF16), 2, 3), adapt_up.astype(BF16)])
    stacked = stack_pieces(gather_rows(packed.reshape(-1, slice_width)))
    stacked = stacked.reshape(devices, 2, sets, projections, rank, slice_width)
    chosen = jnp.sum(adapter_choice * jnp.arange(sets, dtype=jnp.int32)[None, :], axis=1)
    picks = jnp.concatenate([chosen, lax.axis_index("exp").reshape(1)]).astype(jnp.int32)
    factors = pick_sets(stacked, picks, groups)
    mids = jnp.einsum(
        "gsd,gprd->gprs",
        normed.reshape(groups, shard, width),
        factors[:, 0, :3],
        preferred_element_type=F32,
    ).astype(BF16)
    all_mids = lax.all_gather(mids.reshape(groups, 3 * rank, shard), "seq")
    own_ups = lax.dynamic_slice_in_dim(factors[:, 1, :3], here * part, part, axis=3)

    ids = expert_ids.reshape(rows, top)
    gates = gate_weights.reshape(rows, top)
    named = ids.T[:, None, :] == jnp.arange(experts, dtype=jnp.int32)[None, :, None]
    gate_table = jnp.sum(jnp.where(named, gates.T[:, None, :], 0.0), axis=0)
    mask = jnp.any(named, axis=0)
    earlier = jnp.arange(rows)[:, None] < jnp.arange(rows)[None, :]
    ranks = jnp.dot(mask.astype(BF16), earlier.astype(BF16), preferred_element_type=F32)
    slots = jnp.where(mask, ranks, -1.0)
    meta = jnp.stack([slots, gate_table]).reshape(2, devices, local_experts, rows)
    meta = by_relative(lax.all_to_all(jnp.swapaxes(meta, 0, 1), "exp", 0, 0))

    cot_rows = [gather_rows(upstream[g]) for g in range(groups)]
    grad_hidden = expert_grad_hidden(cot_rows, meta, expert_down, capacity)

    saved, attended, mixed, mid_out, moe_rows = [], [], [], [], []
    for g in range(groups):
        att, *kept = attend(
            lengths[g : g + 1],
            raw[g],
            all_mids[:, g],
            own_ups[g],
            query_row,
            key_row,
            cosine,
            sine,
        )
        saved.append(kept)
        attended.append(lax.all_to_all(att, "seq", 0, 0))
        out_mixed, moe_in, mid = project_out(
            attended[g], w_out, factors[g, 0, 3], factors[g, 1, 3], tokens[g], moe_row
        )
        mixed.append(out_mixed)
        mid_out.append(mid)
        moe_rows.append(gather_rows(moe_in))

    hidden, grad_slots = expert_middle(
        moe_rows, meta, expert_gate, expert_up, grad_hidden, capacity
    )
    grad_parts = combine_all(grad_slots, meta, capacity, groups)
    grad_pieces = [scatter_sum(grad_parts[g]) for g in range(groups)]

    produced = expert_produce(hidden, meta, expert_down, capacity)
    out_parts = combine_all(produced, meta, capacity, groups)
    out_pieces = [scatter_sum(out_parts[g]) for g in range(groups)]

    grad_mixed, grad_raw, out_grads = [], [], []
    for g in range(groups):
        gm, grad_att, gdown, gup = project_out_back(
            grad_pieces[g],
            mixed[g],
            upstream[g],
            moe_row,
            w_out,
            factors[g, 0, 3],
            factors[g, 1, 3],
            attended[g],
            mid_out[g],
        )
        grad_mixed.append(gm)
        out_grads.append(jnp.stack([gdown, gup]))
        grad_att = lax.all_to_all(grad_att, "seq", 0, 0)
        back = attend_back(
            lengths[g : g + 1], grad_att, *saved[g], query_row, key_row, cosine, sine
        )
        grad_raw.append(lax.all_to_all(back, "seq", 0, 0))

    outputs = []
    for g in range(groups):
        sums = [mixed[g]]
        for first_row, array in out_pieces[g]:
            after = shard - first_row - array.shape[0]
            sums.append(jnp.pad(array.astype(F32), ((first_row, after), (0, 0))))
        outputs.append(functools.reduce(jnp.add, sums).astype(BF16))
    output = jnp.stack(outputs)

    smalls, grad_down, grad_up = adapter_grads(grad_raw, normed, mids, factors)
    grad_input = project_first_back(
        grad_raw, smalls, factors, w_qkv, flat_tokens, gain_row, grad_mixed
    )

    per_first = jnp.stack([grad_down, grad_up], axis=1)
    per_all = jnp.concatenate([per_first, jnp.stack(out_grads)[:, :, None]], axis=2)
    per_all = per_all.reshape(groups, 2, 4, rank, devices, slice_width)
    came = lax.all_to_all(jnp.moveaxis(per_all, 4, 0), "exp", 0, 0)
    choices = lax.all_gather(adapter_choice.astype(BF16), "exp")
    in_sets = jnp.einsum(
        "dgk,dgcprw->kcprw", choices, came, preferred_element_type=F32
    ).astype(BF16)
    pieces = in_sets.reshape(splits, -1, slice_width)
    pieces = lax.all_to_all(pieces, "seq", 0, 0)
    summed = jnp.sum(pieces.astype(F32), axis=0).astype(BF16)
    summed = lax.all_gather(summed, "seq", axis=0, tiled=True)
    summed = summed.reshape(sets, 2, 4, rank, slice_width).astype(F32)
    shard_down = jnp.swapaxes(summed[:, 0], 2, 3)
    shard_up = summed[:, 1]
    new_first_down, new_second_down, new_down = adam_update(
        adapt_down, shard_down, first_down, second_down, RATE_DOWN
    )
    new_first_up, new_second_up, new_up = adam_update(
        adapt_up, shard_up, first_up, second_up, RATE_UP
    )
    return (
        output,
        grad_input,
        new_first_down,
        new_second_down,
        new_down,
        new_first_up,
        new_second_up,
        new_up,
    )


def solution(mesh):
    in_specs = (
        P("exp", "seq", None),
        P("exp", "seq", None),
        P("exp"),
        P("exp", None),
        P("exp", "seq", None, None, None),
        P("exp", "seq", None, None, None),
        P(),
        P(),
        P(),
        P(),
        P(),
        P(),
        P("exp", None, None),
        P("exp", None, None),
        P("exp", None, None),
        P(None, None, "exp", None),
        P(None, None, "exp", None),
        P(None, None, "exp", None),
        P(None, None, None, "exp"),
        P(None, None, None, "exp"),
        P(None, None, None, "exp"),
    )
    out_specs = (
        P("exp", "seq", None),
        P("exp", "seq", None),
        P(None, None, "exp", None),
        P(None, None, "exp", None),
        P(None, None, "exp", None),
        P(None, None, None, "exp"),
        P(None, None, None, "exp"),
        P(None, None, None, "exp"),
    )
    return jax.shard_map(local, mesh=mesh, in_specs=in_specs, out_specs=out_specs, check_vma=False)
```

time: 1320 us -> 644 us (0.49)
  waiting for transfers between devices: 668 us -> 120 us
  Pallas kernels: 0 us -> 292 us
  matrix products: 248 us -> 2.65 us
  local copies, waits for them, and re-layouts: 223 us -> 39.3 us
  other arithmetic: 132 us -> 35.4 us
  starting transfers between devices: 22.8 us -> 102 us
  blocking collectives: 0 us -> 38.5 us
    pallas_call x0 -> x23, Pallas kernels: none -> 292 us  [the longest x1 77.1 us: expert_middle(): kernel_call(body, 'expert_middle', (experts, steps), [whole_block(meta.sh...]
    all_to_all x4 -> x11, waiting for transfers between devices: 311 us -> 50.5 us  [the longest x2 27.4 us: local(): raw = [lax.all_to_all(first[g], 'seq', 0, 0) for g in range(groups)]]
    dot_general x46 -> x3, matrix products: 248 us -> 2.65 us  [the longest x1 1.83 us: local(): jnp.einsum('gsd,gprd->gprs', normed.reshape(groups, shard, width), factor...]
    all_gather x4 -> x0, waiting for transfers between devices: 159 us -> none  [the longest x1 72.2 us: local(): lax.all_gather(value_rows, 'seq', axis=1, tiled=True)]
    reduce_scatter x3 -> x0, waiting for transfers between devices: 133 us -> none  [the longest x1 74.1 us: local(): lax.psum_scatter(grad_keys_part.astype(jnp.bfloat16), 'seq', scatter_dime...]
    ppermute x0 -> x85, waiting for transfers between devices: none -> 70 us  [swap(): return lax.ppermute(values, 'exp', [(i, i ^ mask) for i in range(count)])]
    ppermute x0 -> x85, starting transfers between devices: none -> 53.8 us  [swap(): return lax.ppermute(values, 'exp', [(i, i ^ mask) for i in range(count)])]
    reshape x6 -> x0, local copies, waits for them, and re-layouts: 45.2 us -> none  [the longest x2 21.5 us: dispatch_rows(): return filled.reshape(local_experts, exp_devices, capacity, model_width)]
  transfers between devices with their start and end apart: 13 -> 96, of which waited for: 13 -> 22; matrix products, arithmetic and copies ran while one was open for 29% -> 11% of each run, Pallas kernels for 0% -> 28%
where the time goes in v1:
time: 644 us; the launch traced here: 633 us
  Pallas kernels  292 us (45%)
  waiting for transfers between devices  120 us (19%)
  starting transfers between devices  102 us (16%)
  local copies, waits for them, and re-layouts  39.3 us (6%)
  blocking collectives  38.5 us (6%)
  other arithmetic  35.4 us (5%)
    pallas_call x1, Pallas kernels, expert_middle(): kernel_call(body, 'expert_middle', (experts, steps), [whole_block(meta.sh...  77.1 us
    ppermute x85, waiting for transfers between devices, swap(): return lax.ppermute(values, 'exp', [(i, i ^ mask) for i in range(count)])  70 us
    ppermute x85, starting transfers between devices, swap(): return lax.ppermute(values, 'exp', [(i, i ^ mask) for i in range(count)])  53.8 us
    pallas_call x8, Pallas kernels, combine(): kernel_call(body, 'combine', (width // block,), [whole_block(meta.shape),...  38 us
    all_to_all x2, waiting for transfers between devices, local(): raw = [lax.all_to_all(first[g], 'seq', 0, 0) for g in range(groups)]  27.4 us
    pallas_call x2, Pallas kernels, attend_back(): kernel_call(body, 'attend_back', (heads,), [pl.BlockSpec((splits, shard,...  26.7 us
    pallas_call x1, Pallas kernels, expert_grad_hidden(): kernel_call(body, 'expert_grad_hidden', (experts,), [whole_block(meta.sha...  26.6 us
    pallas_call x1, Pallas kernels, project_first_back(): kernel_call(body, 'project_first_back', (3, steps), [pl.BlockSpec((groups...  20.6 us
  transfers between devices with their start and end apart: 96, of which 22 were waited for; matrix products, arithmetic and copies ran while one was open for 11% of the time, Pallas kernels for 28%

profile of v1, /device:TPU:0, one launch (start us, length us, event | category | flops | bytes accessed | tf_op | source)
XLA Modules:
  0.0 632.6 jit_solution(7701633222572177416)
XLA Ops:
  0.6 17.1 %project_first.1 = (bf16[4,3,128,512]{3,2,1,0:T(8,128)(2,1)}, bf16[4,3,128,512]{3,2,1,0:T(8,128)(2,1)}, bf16[256,2048]{1,0:T(8,128)(2,1)}) custom-call(bf16[256,2048]{1,0:T(8,128)(2,1)} %bitcast.134, f32[1,2048]{1,0:T(1,128)} %bitcast.163, bf16[3,2048,2048]{2,1,0:T(8,128)(2,1)} %w_ref.15), custom_call_target="tpu_custom_call" | custom-call | flops 6442450944 | bytes 25165824 | tf_op jit(solution)/shard_map/project_first/pallas_call | solution.py:180
  17.8 6.5 %all-to-all-start.3 = ((bf16[4,3,128,512]{3,2,1,0:T(8,128)(2,1)}), bf16[4,3,128,512]{3,2,1,0:T(8,128)(2,1)S(1)}, u32[]{:S(2)}, u32[]{:S(2)}) async-start(bf16[4,3,128,512]{3,2,1,0:T(8,128)(2,1)} %get-tuple-element.79), calls=%async_computation.3 | async-start | bytes 3145728 | tf_op jit(solution)/shard_map/all_to_all | solution.py:853
  33.8 27.4 %all-to-all-done.3.raw_ref = bf16[4,3,128,512]{3,2,1,0:T(8,128)(2,1)S(1)} async-done(((bf16[4,3,128,512]{3,2,1,0:T(8,128)(2,1)}), bf16[4,3,128,512]{3,2,1,0:T(8,128)(2,1)S(1)}, u32[]{:S(2)}, u32[]{:S(2)}) %all-to-all-start.3) | async-done | bytes 1572896 | tf_op jit(solution)/shard_map/all_to_all | solution.py:853
  88.2 9.6 %pick_sets.1.up_ref.down_ref = bf16[2,2,4,16,2048]{4,3,2,1,0:T(8,128)(2,1)} custom-call(s32[3]{0:T(128)} %pad_add_fusion.pick_ref, bf16[8,2,8,4,16,256]{5,4,3,2,1,0:T(8,128)(2,1)} %constant_dynamic-update-slice_fusion.in_ref), custom_call_target="tpu_custom_call" | custom-call | bytes 2097152 | tf_op jit(solution)/shard_map/pick_sets/pallas_call | solution.py:203
  100.7 13.9 %all_gather.12 = bf16[4,2,48,128]{3,2,0,1:T(8,128)(2,1)S(1)} all-gather(bf16[1,2,48,128]{3,2,0,1:T(8,128)(2,1)S(1)} %bitcast.152), channel_id=1, replica_groups=mesh['seq'=4,'exp'=8] {'seq'}, dimensions={0}, use_global_device_ids=true | all-gather | bytes 122880 | tf_op jit(solution)/shard_map/all_gather | solution.py:867
  115.9 9.8 %attend.3 = (bf16[4,128,512]{2,1,0:T(8,128)(2,1)}, bf16[4,512,128]{2,1,0:T(8,128)(2,1)}, bf16[4,512,128]{2,1,0:T(8,128)(2,1)}, bf16[4,512,128]{2,1,0:T(8,128)(2,...) custom-call(s32[1]{0:T(128)} %get-tuple-element.168.len_ref, bf16[4,3,128,512]{3,2,1,0:T(8,128)(2,1)} %copy-done.4, ...), custom_call_target="tpu_custom_call" | custom-call | flops 536870912 | bytes 10485760 | tf_op jit(solution)/shard_map/attend/pallas_call | solution.py:274
  140.3 9.8 %attend.2 = (bf16[4,128,512]{2,1,0:T(8,128)(2,1)}, bf16[4,512,128]{2,1,0:T(8,128)(2,1)}, bf16[4,512,128]{2,1,0:T(8,128)(2,1)}, bf16[4,512,128]{2,1,0:T(8,128)(2,...) custom-call(s32[1]{0:T(128)} %get-tuple-element.169.len_ref, bf16[4,3,128,512]{3,2,1,0:T(8,128)(2,1)} %copy-done.3, ...), custom_call_target="tpu_custom_call" | custom-call | flops 536870912 | bytes 10485760 | tf_op jit(solution)/shard_map/attend/pallas_call | solution.py:274
  158.5 6.9 %project_out.3 = (f32[128,2048]{1,0:T(8,128)}, bf16[128,2048]{1,0:T(8,128)(2,1)}, bf16[16,128]{1,0:T(8,128)(2,1)}) custom-call(bf16[4,128,512]{2,1,0:T(8,128)(2,1)} %copy-done.5, bf16[2048,2048]{1,0:T(8,128)(2,1)} %w_ref.14, bf16[16,2048]{1,0:T(8,128)(2,1)} %get-tuple-element.149.down_ref, bf16[16,2048]{1,0:T(8,128)(2,1)} %get-tuple-element.148.up_ref, ...), custom_call_target="tpu_custom_call" | custom-call | flops 1073741824 | bytes 8388608 | tf_op jit(solution)/shard_map/project_out/pallas_call | solution.py:370
  171.8 6.9 %project_out.2 = (f32[128,2048]{1,0:T(8,128)}, bf16[128,2048]{1,0:T(8,128)(2,1)}, bf16[16,128]{1,0:T(8,128)(2,1)}) custom-call(bf16[4,128,512]{2,1,0:T(8,128)(2,1)} %copy-done.6, bf16[2048,2048]{1,0:T(8,128)(2,1)} %w_ref.14, bf16[16,2048]{1,0:T(8,128)(2,1)} %get-tuple-element.151.down_ref, bf16[16,2048]{1,0:T(8,128)(2,1)} %get-tuple-element.150.up_ref, ...), custom_call_target="tpu_custom_call" | custom-call | flops 1073741824 | bytes 8388608 | tf_op jit(solution)/shard_map/project_out/pallas_call | solution.py:370
  182.7 10.6 %collective-permute-done.27.rest_1_ = bf16[128,2048]{1,0:T(8,128)(2,1)S(1)} collective-permute-done((bf16[128,2048]{1,0:T(8,128)(2,1)}, bf16[128,2048]{1,0:T(8,128)(2,1)S(1)}, u32[]{:S(2)}, u32[]{:S(2)}) %collective-permute-start.27) | collective-permute-done | bytes 524320 | tf_op jit(solution)/shard_map/ppermute | solution.py:101
  211.1 26.6 %expert_grad_hidden.1.gh_ref = bf16[4,768,1024]{2,1,0:T(8,128)(2,1)} custom-call(f32[8,2,4,256]{3,2,1,0:T(4,128)} %broadcast_select_fusion.1.meta_ref, bf16[4,1024,2048]{2,1,0:T(8,128)(2,1)} %w_ref.12, bf16[128,2048]{1,0:T(8,128)(2,1)} %get-tuple-element.153.rest_0_.up_stream_ref, bf16[128,2048]{1,0:T(8,128)(2,1)} %collective-permute-done.9.rest_1_, ...), custom_call_target="tpu_custom_call" | custom-call | flops 16106127360 | bytes 25165824 | tf_op jit(solution)/shard_map/expert_grad_hidden/pallas_call | solution.py:449
  238.8 77.1 %expert_middle.1 = (bf16[4,768,1024]{2,1,0:T(8,128)(2,1)}, bf16[4,768,2048]{2,1,0:T(8,128)(2,1)}) custom-call(f32[8,2,4,256]{3,2,1,0:T(4,128)} %broadcast_select_fusion.1.meta_ref, bf16[4,2048,1024]{2,1,0:T(8,128)(2,1)} %gate_ref.1, bf16[4,2048,1024]{2,1,0:T(8,128)(2,1)} %up_ref.1, bf16[4,768,1024]{2,1,0:T(8,128)(2,1)} %expert_grad_hidden.1.gh_ref, ...), custom_call_target="tpu_custom_call" | custom-call | flops 54760833024 | bytes 58720256 | tf_op jit(solution)/shard_map/expert_middle/pallas_call | solution.py:522
  336.0 19.1 %expert_produce.1.in_ref = bf16[4,768,2048]{2,1,0:T(8,128)(2,1)} custom-call(f32[8,2,4,256]{3,2,1,0:T(4,128)} %broadcast_select_fusion.1.meta_ref, bf16[4,768,1024]{2,1,0:T(8,128)(2,1)} %get-tuple-element.82.h_ref, bf16[4,1024,2048]{2,1,0:T(8,128)(2,1)} %w_ref.12), custom_call_target="tpu_custom_call" | custom-call | flops 12884901888 | bytes 29360128 | tf_op jit(solution)/shard_map/expert_produce/pallas_call | solution.py:565
  370.4 6.8 %collective-permute-done.73 = bf16[64,2048]{1,0:T(8,128)(2,1)S(1)} collective-permute-done((bf16[64,2048]{1,0:T(8,128)(2,1)S(1)}, bf16[64,2048]{1,0:T(8,128)(2,1)S(1)}, u32[]{:S(2)}, u32[]{:S(2)}) %collective-permute-start.73) | collective-permute-done | bytes 262176 | tf_op jit(solution)/shard_map/ppermute | solution.py:101
  387.9 8.8 %project_out_back.3 = (f32[128,2048]{1,0:T(8,128)}, bf16[4,128,512]{2,1,0:T(8,128)(2,1)}, bf16[16,2048]{1,0:T(8,128)(2,1)}, bf16[16,2048]{1,0:T(8,128)(2,1)}) custom-call(f32[128,2048]{1,0:T(8,128)} %get-tuple-element.91.mixed_ref, bf16[128,2048]{1,0:T(8,128)(2,1)} %get-tuple-element.152.rest_10_.up_stream_ref, f32[1,2048]{1,0:T(1,128)} %bitcast.157, ...), custom_call_target="tpu_custom_call" | custom-call | flops 1073741824 | bytes 8388608 | tf_op jit(solution)/shard_map/project_out_back/pallas_call | solution.py:665
  405.8 8.7 %all-gather.1 = bf16[8,2,8]{2,1,0:T(2,128)(2,1)S(1)} all-gather(bf16[1,2,8]{2,1,0:T(2,128)(2,1)S(1)} %get-tuple-element.166), channel_id=2, replica_groups=mesh['seq'=4,'exp'=8] {'exp'}, dimensions={0}, use_global_device_ids=true | all-gather | bytes 288 | tf_op jit(solution)/shard_map/all_gather | solution.py:954
  415.5 8.7 %project_out_back.2 = (f32[128,2048]{1,0:T(8,128)}, bf16[4,128,512]{2,1,0:T(8,128)(2,1)}, bf16[16,2048]{1,0:T(8,128)(2,1)}, bf16[16,2048]{1,0:T(8,128)(2,1)}) custom-call(f32[128,2048]{1,0:T(8,128)} %get-tuple-element.77.mixed_ref, bf16[128,2048]{1,0:T(8,128)(2,1)} %get-tuple-element.153.rest_0_.up_stream_ref, f32[1,2048]{1,0:T(1,128)} %bitcast.158, ...), custom_call_target="tpu_custom_call" | custom-call | flops 1073741824 | bytes 8388608 | tf_op jit(solution)/shard_map/project_out_back/pallas_call | solution.py:665
  445.0 13.4 %attend_back.3 = bf16[4,3,128,512]{3,2,1,0:T(8,128)(2,1)} custom-call(s32[1]{0:T(128)} %get-tuple-element.168.len_ref, bf16[4,128,512]{2,1,0:T(8,128)(2,1)} %copy-done.19, bf16[4,512,128]{2,1,0:T(8,128)(2,1)} %get-tuple-element.126.q_ref, bf16[4,512,128]{2,1,0:T(8,128)(2,1)} %get-tuple-element.127.k_ref, bf16[4,512,128]{2,1,0:T(8,128)(2,1)} %get-tuple-element.128.v_ref, ...), custom_call_target="tpu_custom_call" | custom-call | flops 1342177280 | bytes 14680064 | tf_op jit(solution)/shard_map/attend_back/pallas_call | solution.py:322
  475.6 13.3 %attend_back.2 = bf16[4,3,128,512]{3,2,1,0:T(8,128)(2,1)} custom-call(s32[1]{0:T(128)} %get-tuple-element.169.len_ref, bf16[4,128,512]{2,1,0:T(8,128)(2,1)} %copy-done.18, bf16[4,512,128]{2,1,0:T(8,128)(2,1)} %get-tuple-element.111.q_ref, bf16[4,512,128]{2,1,0:T(8,128)(2,1)} %get-tuple-element.112.k_ref, bf16[4,512,128]{2,1,0:T(8,128)(2,1)} %get-tuple-element.113.v_ref, ...), custom_call_target="tpu_custom_call" | custom-call | flops 1342177280 | bytes 14680064 | tf_op jit(solution)/shard_map/attend_back/pallas_call | solution.py:322
  489.6 12.2 %all-to-all-done.8.rest_1_.rest_3_ = bf16[4,3,128,512]{3,2,1,0:T(8,128)(2,1)S(1)} async-done(((bf16[4,3,128,512]{3,2,1,0:T(8,128)(2,1)}), bf16[4,3,128,512]{3,2,1,0:T(8,128)(2,1)S(1)}, u32[]{:S(2)}, u32[]{:S(2)}) %all-to-all-start.8) | async-done | bytes 1572896 | tf_op jit(solution)/shard_map/all_to_all | solution.py:934
  534.7 7.5 %all-to-all-done.6.rest_0_.rest_2_ = bf16[4,3,128,512]{3,2,1,0:T(8,128)(2,1)S(1)} async-done(((bf16[4,3,128,512]{3,2,1,0:T(8,128)(2,1)}), bf16[4,3,128,512]{3,2,1,0:T(8,128)(2,1)S(1)}, u32[]{:S(2)}, u32[]{:S(2)}) %all-to-all-start.6) | async-done | bytes 1572896 | tf_op jit(solution)/shard_map/all_to_all | solution.py:934
  565.9 13.6 %collective-permute-done.59 = bf16[64,2048]{1,0:T(8,128)(2,1)S(1)} collective-permute-done((bf16[64,2048]{1,0:T(8,128)(2,1)}, bf16[64,2048]{1,0:T(8,128)(2,1)S(1)}, u32[]{:S(2)}, u32[]{:S(2)}) %collective-permute-start.59) | collective-permute-done | bytes 262176 | tf_op jit(solution)/shard_map/ppermute | solution.py:101
  592.5 20.6 %project_first_back.1 = f32[2,128,2048]{2,1,0:T(8,128)} custom-call(bf16[2,3,16,128]{3,2,1,0:T(8,128)(2,1)} %get-tuple-element.131.small_ref, bf16[2,2,4,16,2048]{4,3,2,1,0:T(8,128)(2,1)} %pick_sets.1.up_ref.down_ref, bf16[3,2048,2048]{2,1,0:T(8,128)(2,1)} %w_ref.15, bf16[256,2048]{1,0:T(8,128)(2,1)} %bitcast.135, f32[1,2048]{1,0:T(1,128)} %bitcast.164, ...), custom_call_target="tpu_custom_call" | custom-call | flops 6442450944 | bytes 25165824 | tf_op jit(solution)/shard_map/project_first_back/pallas_call | solution.py:778
  613.2 15.9 %all_gather.15 = bf16[1024,256]{1,0:T(8,128)(2,1)S(1)} all-gather(bf16[256,256]{1,0:T(8,128)(2,1)S(1)} %reduce_sum.32), channel_id=1, replica_groups=mesh['seq'=4,'exp'=8] {'seq'}, dimensions={0}, use_global_device_ids=true | all-gather | bytes 655360 | tf_op jit(solution)/shard_map/all_gather | solution.py:961
  (432 shorter events, 259.5 us)
Async XLA Ops:
  17.8 43.4 %all-to-all-start.3 = ((bf16[4,3,128,512]{3,2,1,0:T(8,128)(2,1)}), bf16[4,3,128,512]{3,2,1,0:T(8,128)(2,1)S(1)}, u32[]{:S(2)}, u32[]{:S(2)}) async-start(bf16[4,3,128,512]{3,2,1,0:T(8,128)(2,1)} %get-tuple-element.79), calls=%async_computation.3 | async-start | bytes 3145728 | tf_op jit(solution)/shard_map/all_to_all | solution.py:853
  25.2 48.4 %collective-permute-start = (bf16[1024,256]{1,0:T(8,128)(2,1)}, bf16[1024,256]{1,0:T(8,128)(2,1)}, u32[]{:S(2)}, u32[]{:S(2)}) collective-permute-start(bf16[1024,256]{1,0:T(8,128)(2,1)} %bitcast.7), channel_id=1, source_target_pairs={{0,1},{1,0},{2,3},{3,2},{4,5},{5,4},{6,7},{7,6},{8,9},{9,8},{10,11... | collective-permute-start | bytes 1572872 | tf_op jit(solution)/shard_map/ppermute | solution.py:101
  25.2 43.2 %collective-permute-start.1 = (bf16[1024,256]{1,0:T(8,128)(2,1)}, bf16[1024,256]{1,0:T(8,128)(2,1)S(1)}, u32[]{:S(2)}, u32[]{:S(2)}) collective-permute-start(bf16[1024,256]{1,0:T(8,128)(2,1)} %bitcast.7), channel_id=1, source_target_pairs={{0,2},{1,3},{2,0},{3,1},{4,6},{5,7},{6,4},{7,5},{8,10},{9,11},{10,... | collective-permute-start | bytes 1572872 | tf_op jit(solution)/shard_map/ppermute | solution.py:101
  26.7 44.1 %collective-permute-start.3 = (bf16[1024,256]{1,0:T(8,128)(2,1)}, bf16[1024,256]{1,0:T(8,128)(2,1)S(1)}, u32[]{:S(2)}, u32[]{:S(2)}) collective-permute-start(bf16[1024,256]{1,0:T(8,128)(2,1)} %bitcast.7), channel_id=1, source_target_pairs={{0,4},{1,5},{2,6},{3,7},{4,0},{5,1},{6,2},{7,3},{8,12},{9,13},{10,... | collective-permute-start | bytes 1572872 | tf_op jit(solution)/shard_map/ppermute | solution.py:101
  30.7 99.6 %collective-permute-start.9 = (bf16[128,2048]{1,0:T(8,128)(2,1)}, bf16[128,2048]{1,0:T(8,128)(2,1)}, u32[]{:S(2)}, u32[]{:S(2)}) collective-permute-start(bf16[128,2048]{1,0:T(8,128)(2,1)} %get-tuple-element.153.rest_0_.up_stream_ref), channel_id=1, source_target_pairs={{0,2},{1,3},{2,0},{3,1},{4,6},{5,7},{6,4},{7,5},{8,10},{9,11},{10,... | collective-permute-start | bytes 1572872 | tf_op jit(solution)/shard_map/ppermute | solution.py:101
  62.4 63.2 %all-to-all-start = ((bf16[4,3,128,512]{3,2,1,0:T(8,128)(2,1)}), bf16[4,3,128,512]{3,2,1,0:T(8,128)(2,1)S(1)}, u32[]{:S(2)}, u32[]{:S(2)}) async-start(bf16[4,3,128,512]{3,2,1,0:T(8,128)(2,1)} %get-tuple-element.74), calls=%async_computation | async-start | bytes 3145728 | tf_op jit(solution)/shard_map/all_to_all | solution.py:853
  78.0 53.3 %collective-permute-start.10 = (bf16[128,2048]{1,0:T(8,128)(2,1)}, bf16[128,2048]{1,0:T(8,128)(2,1)}, u32[]{:S(2)}, u32[]{:S(2)}) collective-permute-start(bf16[128,2048]{1,0:T(8,128)(2,1)} %get-tuple-element.153.rest_0_.up_stream_ref), channel_id=1, source_target_pairs={{0,4},{1,5},{2,6},{3,7},{4,0},{5,1},{6,2},{7,3},{8,12},{9,13},{10,... | collective-permute-start | bytes 1572872 | tf_op jit(solution)/shard_map/ppermute | solution.py:101
  83.6 50.3 %collective-permute-start.18 = (bf16[128,2048]{1,0:T(8,128)(2,1)}, bf16[128,2048]{1,0:T(8,128)(2,1)}, u32[]{:S(2)}, u32[]{:S(2)}) collective-permute-start(bf16[128,2048]{1,0:T(8,128)(2,1)} %get-tuple-element.152.rest_10_.up_stream_ref), channel_id=1, source_target_pairs={{0,2},{1,3},{2,0},{3,1},{4,6},{5,7},{6,4},{7,5},{8,10},{9,11},{10,... | collective-permute-start | bytes 1572872 | tf_op jit(solution)/shard_map/ppermute | solution.py:101
  86.8 48.6 %collective-permute-start.19 = (bf16[128,2048]{1,0:T(8,128)(2,1)}, bf16[128,2048]{1,0:T(8,128)(2,1)}, u32[]{:S(2)}, u32[]{:S(2)}) collective-permute-start(bf16[128,2048]{1,0:T(8,128)(2,1)} %get-tuple-element.152.rest_10_.up_stream_ref), channel_id=1, source_target_pairs={{0,4},{1,5},{2,6},{3,7},{4,0},{5,1},{6,2},{7,3},{8,12},{9,13},{10,... | collective-permute-start | bytes 1572872 | tf_op jit(solution)/shard_map/ppermute | solution.py:101
  87.3 50.4 %collective-permute-start.13 = (bf16[128,2048]{1,0:T(8,128)(2,1)}, bf16[128,2048]{1,0:T(8,128)(2,1)}, u32[]{:S(2)}, u32[]{:S(2)}) collective-permute-start(bf16[128,2048]{1,0:T(8,128)(2,1)} %get-tuple-element.153.rest_0_.up_stream_ref), channel_id=1, source_target_pairs={{0,1},{1,0},{2,3},{3,2},{4,5},{5,4},{6,7},{7,6},{8,9},{9,8},{10,11... | collective-permute-start | bytes 1572872 | tf_op jit(solution)/shard_map/ppermute | solution.py:101
  335.5 34.2 %collective-permute-start.75 = (bf16[128,2048]{1,0:T(8,128)(2,1)}, bf16[128,2048]{1,0:T(8,128)(2,1)S(1)}, u32[]{:S(2)}, u32[]{:S(2)}) collective-permute-start(bf16[128,2048]{1,0:T(8,128)(2,1)} %get-tuple-element.118), channel_id=1, source_target_pairs={{0,1},{1,0},{2,3},{3,2},{4,5},{5,4},{6,7},{7,6},{8,9},{9,8},{10,11... | collective-permute-start | bytes 1572872 | tf_op jit(solution)/shard_map/ppermute | solution.py:101
  368.2 31.9 %collective-permute-start.71 = (bf16[64,2048]{1,0:T(8,128)(2,1)}, bf16[64,2048]{1,0:T(8,128)(2,1)S(1)}, u32[]{:S(2)}, u32[]{:S(2)}) collective-permute-start(bf16[64,2048]{1,0:T(8,128)(2,1)} %get-tuple-element.157), channel_id=1, source_target_pairs={{0,2},{1,3},{2,0},{3,1},{4,6},{5,7},{6,4},{7,5},{8,10},{9,11},{10,... | collective-permute-start | bytes 786440 | tf_op jit(solution)/shard_map/ppermute | solution.py:101
  377.7 36.7 %collective-permute-start.69 = (bf16[64,2048]{1,0:T(8,128)(2,1)}, bf16[64,2048]{1,0:T(8,128)(2,1)S(1)}, u32[]{:S(2)}, u32[]{:S(2)}) collective-permute-start(bf16[64,2048]{1,0:T(8,128)(2,1)} %slice.253), channel_id=1, source_target_pairs={{0,4},{1,5},{2,6},{3,7},{4,0},{5,1},{6,2},{7,3},{8,12},{9,13},{10,... | collective-permute-start | bytes 786440 | tf_op jit(solution)/shard_map/ppermute | solution.py:101
  405.7 39.1 %collective-permute-start.48 = (bf16[128,2048]{1,0:T(8,128)(2,1)}, bf16[128,2048]{1,0:T(8,128)(2,1)S(1)}, u32[]{:S(2)}, u32[]{:S(2)}) collective-permute-start(bf16[128,2048]{1,0:T(8,128)(2,1)} %get-tuple-element.88), channel_id=1, source_target_pairs={{0,1},{1,0},{2,3},{3,2},{4,5},{5,4},{6,7},{7,6},{8,9},{9,8},{10,11... | collective-permute-start | bytes 1572872 | tf_op jit(solution)/shard_map/ppermute | solution.py:101
  424.2 34.7 %all-to-all-start.5 = ((bf16[4,128,512]{2,1,0:T(8,128)(2,1)}), bf16[4,128,512]{2,1,0:T(8,128)(2,1)S(1)}, u32[]{:S(2)}, u32[]{:S(2)}) async-start(bf16[4,128,512]{2,1,0:T(8,128)(2,1)} %get-tuple-element.110), calls=%async_computation.5 | async-start | bytes 1048576 | tf_op jit(solution)/shard_map/all_to_all | solution.py:930
  444.3 108.0 %collective-permute-start.45 = (bf16[128,2048]{1,0:T(8,128)(2,1)}, bf16[128,2048]{1,0:T(8,128)(2,1)}, u32[]{:S(2)}, u32[]{:S(2)}) collective-permute-start(bf16[128,2048]{1,0:T(8,128)(2,1)} %get-tuple-element.84), channel_id=1, source_target_pairs={{0,1},{1,0},{2,3},{3,2},{4,5},{5,4},{6,7},{7,6},{8,9},{9,8},{10,11... | collective-permute-start | bytes 1572872 | tf_op jit(solution)/shard_map/ppermute | solution.py:101
  459.2 42.6 %all-to-all-start.8 = ((bf16[4,3,128,512]{3,2,1,0:T(8,128)(2,1)}), bf16[4,3,128,512]{3,2,1,0:T(8,128)(2,1)S(1)}, u32[]{:S(2)}, u32[]{:S(2)}) async-start(bf16[4,3,128,512]{3,2,1,0:T(8,128)(2,1)} %attend_back.3), calls=%async_computation.8 | async-start | bytes 3145728 | tf_op jit(solution)/shard_map/all_to_all | solution.py:934
  465.7 100.2 %collective-permute-start.55 = (bf16[128,2048]{1,0:T(8,128)(2,1)}, bf16[128,2048]{1,0:T(8,128)(2,1)}, u32[]{:S(2)}, u32[]{:S(2)}) collective-permute-start(bf16[128,2048]{1,0:T(8,128)(2,1)} %get-tuple-element.93), channel_id=1, source_target_pairs={{0,1},{1,0},{2,3},{3,2},{4,5},{5,4},{6,7},{7,6},{8,9},{9,8},{10,11... | collective-permute-start | bytes 1572872 | tf_op jit(solution)/shard_map/ppermute | solution.py:101
  469.6 89.4 %collective-permute-start.49 = (bf16[64,2048]{1,0:T(8,128)(2,1)}, bf16[64,2048]{1,0:T(8,128)(2,1)}, u32[]{:S(2)}, u32[]{:S(2)}) collective-permute-start(bf16[64,2048]{1,0:T(8,128)(2,1)} %slice.241), channel_id=1, source_target_pairs={{0,4},{1,5},{2,6},{3,7},{4,0},{5,1},{6,2},{7,3},{8,12},{9,13},{10,... | collective-permute-start | bytes 786440 | tf_op jit(solution)/shard_map/ppermute | solution.py:101
  472.3 38.2 %collective-permute-start.51 = (bf16[64,2048]{1,0:T(8,128)(2,1)}, bf16[64,2048]{1,0:T(8,128)(2,1)S(1)}, u32[]{:S(2)}, u32[]{:S(2)}) collective-permute-start(bf16[64,2048]{1,0:T(8,128)(2,1)} %get-tuple-element.158), channel_id=1, source_target_pairs={{0,2},{1,3},{2,0},{3,1},{4,6},{5,7},{6,4},{7,5},{8,10},{9,11},{10,... | collective-permute-start | bytes 786440 | tf_op jit(solution)/shard_map/ppermute | solution.py:101
  488.9 72.2 %collective-permute-start.47 = (bf16[64,2048]{1,0:T(8,128)(2,1)}, bf16[64,2048]{1,0:T(8,128)(2,1)}, u32[]{:S(2)}, u32[]{:S(2)}) collective-permute-start(bf16[64,2048]{1,0:T(8,128)(2,1)} %slice.240), channel_id=1, source_target_pairs={{0,2},{1,3},{2,0},{3,1},{4,6},{5,7},{6,4},{7,5},{8,10},{9,11},{10,... | collective-permute-start | bytes 786440 | tf_op jit(solution)/shard_map/ppermute | solution.py:101
  501.9 40.3 %all-to-all-start.6 = ((bf16[4,3,128,512]{3,2,1,0:T(8,128)(2,1)}), bf16[4,3,128,512]{3,2,1,0:T(8,128)(2,1)S(1)}, u32[]{:S(2)}, u32[]{:S(2)}) async-start(bf16[4,3,128,512]{3,2,1,0:T(8,128)(2,1)} %attend_back.2), calls=%async_computation.6 | async-start | bytes 3145728 | tf_op jit(solution)/shard_map/all_to_all | solution.py:934
  532.0 30.6 %collective-permute-start.52 = (bf16[64,2048]{1,0:T(8,128)(2,1)}, bf16[64,2048]{1,0:T(8,128)(2,1)}, u32[]{:S(2)}, u32[]{:S(2)}) collective-permute-start(bf16[64,2048]{1,0:T(8,128)(2,1)} %add_convert_fusion.21), channel_id=1, source_target_pairs={{0,4},{1,5},{2,6},{3,7},{4,0},{5,1},{6,2},{7,3},{8,12},{9,13},{10,... | collective-permute-start | bytes 786440 | tf_op jit(solution)/shard_map/ppermute | solution.py:101
  555.3 31.1 %all-to-all-start.9 = ((bf16[8,2,2,4,16,256]{5,1,4,3,2,0:T(2,128)(2,1)}), bf16[8,2,2,4,16,256]{5,1,4,3,2,0:T(2,128)(2,1)S(1)}, u32[]{:S(2)}, u32[]{:S(2)}) async-start(bf16[8,2,2,4,16,256]{5,1,4,3,2,0:T(2,128)(2,1)} %maximum_bitcast_fusion), calls=%async_computation.9 | async-start | bytes 2097152 | tf_op jit(solution)/shard_map/all_to_all | solution.py:953
  (139 other events, 2246.5 us)
